TPU v7x, 32 devices: a whole 2x2x4 slice. The times are simulated.
32 devices in a mesh: dp: 8 (over z, y), chan: 4 (over x, core).
Axes of the slice: x: 2, y: 2, z: 4, core: 2. Of those that a mesh axis runs over, the one named last changes fastest.
Arguments:
- x_in: float32 [1024, 1024], P('dp', 'chan'), may hold values from -6 to 6
- norm_gain: float32 [2, 1024], P(None, 'chan'), may hold values from 0.5 to 1.5
- in_weight: bfloat16 [2, 1024, 2, 2048], P(None, None, None, 'chan'), may hold values from -0.1875 to 0.1875
- conv_weight: float32 [2, 4, 2048], P(None, None, 'chan'), may hold values from -3 to 3
- conv_bias: float32 [2, 2048], P(None, 'chan'), may hold values from -1.5 to 1.5
- xproj_weight: bfloat16 [2, 96, 2048], P(None, None, 'chan'), may hold values from -0.125 to 0.125
- dt_weight: bfloat16 [2, 64, 2048], P(None, None, 'chan'), may hold values from -0.75 to 0.75
- dt_bias: float32 [2, 2048], P(None, 'chan'), may hold values from -3 to -1
- a_log: float32 [2, 16, 2048], P(None, None, 'chan'), may hold values from -7 to 1.5
- skip_gain: float32 [2, 2048], P(None, 'chan'), may hold values from 0.5 to 1.5
- out_weight: bfloat16 [2, 2048, 1024], P(None, 'chan'), may hold values from -0.125 to 0.125
- seq_lengths: int32 [4], replicated, may hold values from 1 to 897, 1024 in all
- char_mask: int32 [1024], P('dp'), may hold values 0 or 1
- out_probe: float32 [1024, 1024], P('dp', 'chan'), may hold values from -6 to 6
Outputs:
- block_out: float32 [1024, 1024], P('dp', 'chan')
- input_grad: float32 [1024, 1024], P('dp', 'chan')
- gain_grad: float32 [2, 1024], P(None, 'chan')
- in_weight_grad: float32 [2, 1024, 2, 2048], P(None, None, None, 'chan')
- conv_weight_grad: float32 [2, 4, 2048], P(None, None, 'chan')
- conv_bias_grad: float32 [2, 2048], P(None, 'chan')
- xproj_grad: float32 [2, 96, 2048], P(None, None, 'chan')
- dt_weight_grad: float32 [2, 64, 2048], P(None, None, 'chan')
- dt_bias_grad: float32 [2, 2048], P(None, 'chan')
- a_log_grad: float32 [2, 16, 2048], P(None, None, 'chan')
- skip_grad: float32 [2, 2048], P(None, 'chan')
- out_weight_grad: float32 [2, 2048, 1024], P(None, 'chan')
Inputs may be any that keep to these rules, and one draw needn't show every extreme that they name: `seq_lengths`: the lengths sum to 1024; the longest is exactly 897.
All inputs are finite; a program needn't handle non-finite values. No bound on the sum of `char_mask` on one device may be relied on, other than what follows from the above.
Results may differ from a plain program's by a relative error of at most 0.02.
Values may be sent and summed in bfloat16 or wider, within the bound.
A program may use at most 192 MiB of HBM per device.

v0:
```python
import jax
import jax.numpy as jnp
from jax import lax
from jax.sharding import PartitionSpec as P

D = 1024
STATE = 16
CONV = 4
RANK = 64
LAYERS = 2


epsilon = 1e-05


def from_behind(value, axis, steps):
    count = lax.axis_size(axis)
    initial, last = (max(0, -steps), min(count, count - steps))
    return lax.ppermute(value, axis, [(source, source + steps) for source in range(initial, last)])


def carried_in(value, axis, join, neutral):
    count, mine = (lax.axis_size(axis), lax.axis_index(axis))
    pieces = jax.tree.map(lambda part: lax.all_gather(part, axis), value)
    subtotal = jax.tree.map(
        lambda part, zero: jnp.full_like(part, 0) + jnp.asarray(zero, part.dtype), value, neutral
    )

    def carried_lap(position, subtotal):
        longer = join(subtotal, jax.tree.map(lambda part: part[position], pieces))
        return jax.tree.map(lambda new, old: jnp.where(position < mine, new, old), longer, subtotal)

    return lax.fori_loop(0, count - 1, carried_lap, subtotal)


def prefix(shard, axis, combine, identity):
    devices, place = (lax.axis_size(axis), lax.axis_index(axis))
    everything = jax.tree.map(
        lambda part, kind: lax.all_gather(part.astype(kind), axis),
        shard,
        (jnp.bfloat16, jnp.bfloat16),
    )
    start = jax.tree.map(
        lambda part, zero: jnp.broadcast_to(jnp.asarray(zero, part.dtype), part.shape),
        shard,
        identity,
    )

    def prefix_lap(k, before):
        at = devices - 1 - k
        reached = at > place
        new = combine(
            before, jax.tree.map(lambda part, own: part[at].astype(own.dtype), everything, shard)
        )
        return jax.tree.map(lambda a, b: jnp.where(reached, a, b), new, before)

    return lax.fori_loop(0, devices, prefix_lap, start)


def chain_pair(former, latter):
    return (former[0] * latter[0], latter[0] * former[1] + latter[1])


def silu_slope(value):
    sigmoid_v = jax.nn.sigmoid(value)
    return sigmoid_v * (1.0 + value * (1.0 - sigmoid_v))


def block_scan(decays, drives):
    tok_rows = decays.shape[0]
    span = min(32, tok_rows)
    count = tok_rows // span
    tail = decays.shape[1:]
    dec_blocks = decays.reshape((count, span) + tail)
    drv_blocks = drives.reshape((count, span) + tail)
    prod_in, acc_in = lax.associative_scan(chain_pair, (dec_blocks, drv_blocks), axis=1)

    def link(carry, item):
        prev_prod, prev_acc = carry
        block_prod, block_acc = item
        joined_prod = block_prod * prev_prod[None]
        joined_acc = block_acc + block_prod * prev_acc[None]
        return ((joined_prod[-1], joined_acc[-1]), (joined_prod, joined_acc))

    start = (jnp.ones(tail, jnp.float32), jnp.zeros(tail, jnp.float32))
    last_pair, joined = lax.scan(link, start, (prod_in, acc_in))
    return (joined[0].reshape(decays.shape), joined[1].reshape(decays.shape))


def local_scan(step_size, act_float, b_matrix, a_matrix, keeping):
    decays = jnp.exp(step_size[:, None, :] * a_matrix[None]) * keeping[:, None, None]
    drives = (step_size * act_float)[:, None, :] * b_matrix[:, :, None]
    decay_prod, local_sum = block_scan(decays, drives)
    return (decays, decay_prod, local_sum)


def conv_apply(padded, w_conv, b_conv, conv_taps, tok_rows):
    conv_out = jnp.zeros((tok_rows, padded.shape[1]), jnp.float32) + b_conv[None, :]
    for tap_index in range(CONV):
        conv_out = (
            conv_out
            + w_conv[tap_index][None, :]
            * padded[tap_index : tap_index + tok_rows]
            * conv_taps[tap_index]
        )
    return conv_out


def layer_forward(stream, params, keeping, conv_taps):
    gain_row, w_in, w_conv, b_conv, w_x, w_dt, b_dt, a_row, skip_row, w_out = params
    tok_rows = stream.shape[0]
    chan_width = w_in.shape[2]
    rim_rows = CONV - 1
    squares = lax.psum(jnp.sum(stream * stream, axis=1), "chan")
    inv_rms = lax.rsqrt(squares / D + epsilon)
    hidden = (stream * inv_rms[:, None] * gain_row[None, :]).astype(jnp.bfloat16)
    gathered = lax.all_gather(hidden, "chan", axis=1, tiled=True)
    mixed_rows = jnp.dot(
        gathered, w_in.reshape(w_in.shape[0], 2 * chan_width), preferred_element_type=jnp.float32
    ).astype(jnp.bfloat16)
    inner_in = mixed_rows[:, :chan_width]
    gate_in = mixed_rows[:, chan_width:].astype(jnp.float32)
    before = from_behind(inner_in[tok_rows - rim_rows :], "dp", 1)
    padded = jnp.concatenate([before, inner_in], axis=0).astype(jnp.float32)
    conv_out = conv_apply(padded, w_conv, b_conv, conv_taps, tok_rows)
    activated = jax.nn.silu(conv_out).astype(jnp.bfloat16)
    act_float = activated.astype(jnp.float32)
    low_part = jnp.einsum("te,ke->tk", activated, w_x, preferred_element_type=jnp.float32)
    projected = lax.psum(low_part, "chan")
    step_in = projected[:, :RANK].astype(jnp.bfloat16)
    b_matrix = projected[:, RANK : RANK + STATE]
    c_matrix = projected[:, RANK + STATE :]
    step_pre = jnp.dot(step_in, w_dt, preferred_element_type=jnp.float32) + b_dt[None, :]
    step_size = jax.nn.softplus(step_pre)
    a_matrix = -jnp.exp(a_row)
    decays, decay_prod, local_sum = local_scan(step_size, act_float, b_matrix, a_matrix, keeping)
    carry_in = carried_in(
        (decay_prod[-1], local_sum[-1]),
        "dp",
        chain_pair,
        (jnp.ones_like(decay_prod[-1]), jnp.zeros_like(local_sum[-1])),
    )[1]
    states = local_sum + decay_prod * carry_in[None]
    scanned = jnp.sum(c_matrix[:, :, None] * states, axis=1) + skip_row[None, :] * act_float
    gated_rows = (scanned * jax.nn.silu(gate_in)).astype(jnp.bfloat16)
    out_terms = jnp.dot(gated_rows, w_out, preferred_element_type=jnp.float32)
    branch = lax.psum_scatter(out_terms, "chan", scatter_dimension=1, tiled=True)
    stored = (
        stream,
        inv_rms,
        gathered,
        before,
        inner_in,
        gate_in,
        activated,
        projected,
        step_in,
        step_pre,
        carry_in,
        scanned,
        gated_rows,
    )
    return (stream + branch, stored)


def layer_backward(cotangent, params, stored, keeping, conv_taps):
    gain_row, w_in, w_conv, b_conv, w_x, w_dt, b_dt, a_row, skip_row, w_out = params
    (
        stream,
        inv_rms,
        gathered,
        before,
        inner_in,
        gate_in,
        activated,
        projected,
        step_in,
        step_pre,
        carry_in,
        scanned,
        gated_rows,
    ) = stored
    tok_rows = stream.shape[0]
    chan_width = w_in.shape[2]
    rim_rows = CONV - 1
    act_float = activated.astype(jnp.float32)
    b_matrix = projected[:, RANK : RANK + STATE]
    c_matrix = projected[:, RANK + STATE :]
    step_size = jax.nn.softplus(step_pre)
    a_matrix = -jnp.exp(a_row)
    decays, decay_prod, local_sum = local_scan(step_size, act_float, b_matrix, a_matrix, keeping)
    states = local_sum + decay_prod * carry_in[None]
    grad_low = cotangent.astype(jnp.bfloat16)
    grad_full = lax.all_gather(grad_low, "chan", axis=1, tiled=True)
    grad_out_w = jnp.einsum("te,td->ed", gated_rows, grad_full, preferred_element_type=jnp.float32)
    grad_gated = jnp.einsum("td,ed->te", grad_full, w_out, preferred_element_type=jnp.float32)
    grad_scan = grad_gated * jax.nn.silu(gate_in)
    grad_gate_in = grad_gated * scanned * silu_slope(gate_in)
    grad_skip = jnp.sum(grad_scan * act_float, axis=0)
    grad_act = grad_scan * skip_row[None, :]
    grad_states = c_matrix[:, :, None] * grad_scan[:, None, :]
    grad_cmat = jnp.sum(grad_scan[:, None, :] * states, axis=2)
    rev_prod, rev_sum = block_scan(decays[::-1], (decays * grad_states)[::-1])
    rev_prod = rev_prod[::-1]
    rev_sum = rev_sum[::-1]
    from_above = prefix(
        (rev_prod[0], rev_sum[0]),
        "dp",
        chain_pair,
        (jnp.ones_like(rev_prod[0]), jnp.zeros_like(rev_sum[0])),
    )[1]
    flowing = rev_sum + rev_prod * from_above[None]
    adjoint = grad_states + jnp.concatenate([flowing[1:], from_above[None]], axis=0)
    earlier = jnp.concatenate([carry_in[None], states[:-1]], axis=0)
    grad_rate = adjoint * earlier * decays
    adjoint_b = jnp.sum(adjoint * b_matrix[:, :, None], axis=1)
    grad_step = jnp.sum(grad_rate * a_matrix[None], axis=1) + adjoint_b * act_float
    grad_a_log = jnp.sum(grad_rate * step_size[:, None, :], axis=0) * a_matrix
    grad_act = grad_act + step_size * adjoint_b
    grad_bmat = jnp.sum(adjoint * (step_size * act_float)[:, None, :], axis=2)
    grad_pre = grad_step * jax.nn.sigmoid(step_pre)
    grad_bias = jnp.sum(grad_pre, axis=0)
    pre_low = grad_pre.astype(jnp.bfloat16)
    grad_dt_w = jnp.einsum("tr,te->re", step_in, pre_low, preferred_element_type=jnp.float32)
    grad_step_in = jnp.einsum("te,re->tr", pre_low, w_dt, preferred_element_type=jnp.float32)
    back_part = jnp.concatenate([grad_step_in, grad_bmat, grad_cmat], axis=1)
    grad_proj = lax.psum(back_part, "chan").astype(jnp.bfloat16)
    grad_x_w = jnp.einsum("tk,te->ke", grad_proj, activated, preferred_element_type=jnp.float32)
    grad_act = grad_act + jnp.einsum(
        "tk,ke->te", grad_proj, w_x, preferred_element_type=jnp.float32
    )
    padded = jnp.concatenate([before, inner_in], axis=0).astype(jnp.float32)
    conv_out = conv_apply(padded, w_conv, b_conv, conv_taps, tok_rows)
    grad_conv = grad_act * silu_slope(conv_out)
    grad_conv_b = jnp.sum(grad_conv, axis=0)
    grad_conv_w = jnp.stack(
        [
            jnp.sum(
                grad_conv * conv_taps[tap_index] * padded[tap_index : tap_index + tok_rows], axis=0
            )
            for tap_index in range(CONV)
        ]
    )
    grad_padded = jnp.zeros((tok_rows + rim_rows, chan_width), jnp.float32)
    for tap_index in range(CONV):
        grad_padded = grad_padded + jnp.pad(
            grad_conv * conv_taps[tap_index] * w_conv[tap_index][None, :],
            ((tap_index, rim_rows - tap_index), (0, 0)),
        )
    returned = from_behind(grad_padded[:rim_rows], "dp", -1)
    grad_inner = grad_padded[rim_rows:] + jnp.pad(returned, ((tok_rows - rim_rows, 0), (0, 0)))
    grad_mixed = jnp.concatenate([grad_inner, grad_gate_in], axis=1).astype(jnp.bfloat16)
    grad_in_w = jnp.einsum(
        "td,tk->dk", gathered, grad_mixed, preferred_element_type=jnp.float32
    ).reshape(w_in.shape)
    hidden_part = jnp.einsum(
        "tk,dk->td",
        grad_mixed,
        w_in.reshape(w_in.shape[0], 2 * chan_width),
        preferred_element_type=jnp.float32,
    )
    grad_hidden = lax.psum_scatter(
        hidden_part.astype(jnp.bfloat16), "chan", scatter_dimension=1, tiled=True
    ).astype(jnp.float32)
    normed = stream * inv_rms[:, None]
    grad_gain = jnp.sum(grad_hidden * normed, axis=0)
    grad_normed = grad_hidden * gain_row[None, :]
    row_dot = lax.psum(jnp.sum(grad_normed * normed, axis=1), "chan")
    grad_stream = cotangent + inv_rms[:, None] * (grad_normed - normed * (row_dot / D)[:, None])
    return (
        grad_stream,
        (
            grad_gain,
            grad_in_w,
            grad_conv_w,
            grad_conv_b,
            grad_x_w,
            grad_dt_w,
            grad_bias,
            grad_a_log,
            grad_skip,
            grad_out_w,
        ),
    )


def local(
    x_in,
    norm_gain,
    in_weight,
    conv_weight,
    conv_bias,
    xproj_weight,
    dt_weight,
    dt_bias,
    a_log,
    skip_gain,
    out_weight,
    seq_lengths,
    char_mask,
    out_probe,
):
    tok_rows = x_in.shape[0]
    dev_place = lax.axis_index("dp")
    starts = jnp.cumsum(seq_lengths) - seq_lengths
    positions = dev_place * tok_rows + jnp.arange(tok_rows, dtype=jnp.int32)
    seq_first = jnp.max(
        jnp.where(starts[None, :] <= positions[:, None], starts[None, :], 0), axis=1
    )
    offset = positions - seq_first
    keeping = (offset > 0).astype(jnp.float32)
    conv_taps = [
        (offset >= CONV - 1 - tap_index).astype(jnp.float32)[:, None] for tap_index in range(CONV)
    ]
    layer_params = [
        (
            norm_gain[layer_index],
            in_weight[layer_index],
            conv_weight[layer_index],
            conv_bias[layer_index],
            xproj_weight[layer_index],
            dt_weight[layer_index],
            dt_bias[layer_index],
            a_log[layer_index],
            skip_gain[layer_index],
            out_weight[layer_index],
        )
        for layer_index in range(LAYERS)
    ]
    stream = x_in
    kept_list = []
    for layer_index in range(LAYERS):
        stream, stored = layer_forward(stream, layer_params[layer_index], keeping, conv_taps)
        kept_list.append(stored)
    cotangent = out_probe * char_mask.astype(jnp.float32)[:, None]
    grad_list = []
    for layer_index in reversed(range(LAYERS)):
        cotangent, layer_grads = layer_backward(
            cotangent, layer_params[layer_index], kept_list[layer_index], keeping, conv_taps
        )
        g_gain, g_in, g_conv_w, g_conv_b, g_x, g_dt, g_bias, g_alog, g_skip, g_out = layer_grads
        layer_grads = lax.psum(
            (g_gain, g_in, g_conv_w, g_conv_b, g_x, g_dt, g_bias, g_alog, g_skip, g_out), "dp"
        )
        grad_list.insert(0, layer_grads)
    stacked = [jnp.stack([grads_of[member] for grads_of in grad_list]) for member in range(10)]
    s_gain, s_in, s_conv_w, s_conv_b, s_x, s_dt, s_bias, s_alog, s_skip, s_out = stacked
    return (
        stream,
        cotangent,
        s_gain,
        s_in,
        s_conv_w,
        s_conv_b,
        s_x,
        s_dt,
        s_bias,
        s_alog,
        s_skip,
        s_out,
    )


def solution(mesh):
    return jax.shard_map(
        local,
        mesh=mesh,
        in_specs=(
            P("dp", "chan"),
            P(None, "chan"),
            P(None, None, None, "chan"),
            P(None, None, "chan"),
            P(None, "chan"),
            P(None, None, "chan"),
            P(None, None, "chan"),
            P(None, "chan"),
            P(None, None, "chan"),
            P(None, "chan"),
            P(None, "chan", None),
            P(),
            P("dp"),
            P("dp", "chan"),
        ),
        out_specs=(
            P("dp", "chan"),
            P("dp", "chan"),
            P(None, "chan"),
            P(None, None, None, "chan"),
            P(None, None, "chan"),
            P(None, "chan"),
            P(None, None, "chan"),
            P(None, None, "chan"),
            P(None, "chan"),
            P(None, None, "chan"),
            P(None, "chan"),
            P(None, "chan", None),
        ),
        check_vma=False,
    )
```

profile of v0, /device:TPU:1, one launch (start us, length us, event | category | flops | bytes accessed | tf_op | source)
XLA Modules:
  0.0 2193.3 jit_solution(4691972171264835586)
XLA Ops:
  139.3 12.4 pad.339
  151.6 11.2 pad.340
  167.3 16.6 pad.329
  184.0 11.2 pad.330
  205.7 21.7 pad.342
  229.1 21.7 pad.341
  257.8 21.7 pad.332
  281.3 21.9 pad.331
  315.2 13.3 while.138
  329.2 24.8 %all_gather.41 = f32[8,16,512]{2,1,0:T(8,128)S(1)} all-gather(f32[1,16,512]{2,1,0:T(8,128)S(1)} %slice.1221), channel_id=1, replica_groups=mesh['dp'=8,'chan'=4] {'dp'}, dimensions={0}, use_global_device_ids=true | all-gather | bytes 294912 | tf_op jit(solution)/shard_map/all_gather | solution.py:24
  354.8 25.1 %all_gather.42 = f32[8,16,512]{2,1,0:T(8,128)S(1)} all-gather(f32[1,16,512]{2,1,0:T(8,128)S(1)} %slice.1222), channel_id=1, replica_groups=mesh['dp'=8,'chan'=4] {'dp'}, dimensions={0}, use_global_device_ids=true | all-gather | bytes 294912 | tf_op jit(solution)/shard_map/all_gather | solution.py:24
  388.8 31.0 %reduce-scatter.5.cloned.1.call-done = f32[128,256]{1,0:T(8,128)} async-done(((f32[128,1024]{1,0:T(8,128)}), f32[128,256]{1,0:T(8,128)}) %reduce-scatter.5.cloned.1.call-update) | async-done | bytes 131088 | tf_op jit(solution)/shard_map/reduce_scatter | solution.py:147
  545.4 12.4 pad.359
  557.8 11.1 pad.360
  573.4 16.6 pad.349
  711.6 12.4 pad.379
  739.5 16.6 pad.369
  777.4 21.4 pad.382
  800.6 21.2 pad.381
  828.8 21.4 pad.372
  851.9 21.2 pad.371
  885.1 13.6 while.140
  910.4 21.3 pad.362
  933.4 21.2 pad.361
  961.6 21.5 pad.352
  984.9 21.6 pad.351
  1018.5 13.5 while.139
  1032.8 24.5 %all_gather.44 = f32[8,16,512]{2,1,0:T(8,128)S(1)} all-gather(f32[1,16,512]{2,1,0:T(8,128)S(1)} %slice.1263), channel_id=1, replica_groups=mesh['dp'=8,'chan'=4] {'dp'}, dimensions={0}, use_global_device_ids=true | all-gather | bytes 294912 | tf_op jit(solution)/shard_map/all_gather | solution.py:24
  1058.1 24.6 %all_gather.45 = f32[8,16,512]{2,1,0:T(8,128)S(1)} all-gather(f32[1,16,512]{2,1,0:T(8,128)S(1)} %slice.1264), channel_id=1, replica_groups=mesh['dp'=8,'chan'=4] {'dp'}, dimensions={0}, use_global_device_ids=true | all-gather | bytes 294912 | tf_op jit(solution)/shard_map/all_gather | solution.py:24
  1089.8 24.4 %all_gather.47 = bf16[8,16,512]{2,1,0:T(8,128)(2,1)S(1)} all-gather(bf16[1,16,512]{2,1,0:T(8,128)(2,1)S(1)} %slice.1745), channel_id=1, replica_groups=mesh['dp'=8,'chan'=4] {'dp'}, dimensions={0}, use_global_device_ids=true | all-gather | bytes 147456 | tf_op jit(solution)/shard_map/all_gather | solution.py:39
  1114.2 24.5 %all_gather.48 = bf16[8,16,512]{2,1,0:T(8,128)(2,1)S(1)} all-gather(bf16[1,16,512]{2,1,0:T(8,128)(2,1)S(1)} %slice.1744), channel_id=1, replica_groups=mesh['dp'=8,'chan'=4] {'dp'}, dimensions={0}, use_global_device_ids=true | all-gather | bytes 147456 | tf_op jit(solution)/shard_map/all_gather | solution.py:39
  1154.9 36.3 %psum.200 = bf16[128,96]{0,1:T(8,128)(2,1)S(1)} all-reduce(f32[128,96]{0,1:T(8,128)S(1)} %pad_maximum_fusion.43), channel_id=1, replica_groups=mesh['dp'=8,'chan'=4] {'chan'}, use_global_device_ids=true, to_apply=%region_28.29 | all-reduce | flops 12288 | bytes 73728 | tf_op jit(solution)/shard_map/psum | solution.py:227
  1230.5 11.2 reduce-scatter.7.cloned.1.call-done
  1353.0 12.4 pad.404
  1365.3 11.2 pad.405
  1381.1 16.7 pad.394
  1397.8 11.1 pad.395
  1419.3 21.7 pad.407
  1442.8 21.7 pad.406
  1471.6 21.7 pad.397
  1495.0 21.8 pad.396
  1528.9 13.4 while.141
  1554.0 24.2 %all_gather.50 = bf16[8,16,512]{2,1,0:T(8,128)(2,1)S(1)} all-gather(bf16[1,16,512]{2,1,0:T(8,128)(2,1)S(1)} %slice.1743), channel_id=1, replica_groups=mesh['dp'=8,'chan'=4] {'dp'}, dimensions={0}, use_global_device_ids=true | all-gather | bytes 147456 | tf_op jit(solution)/shard_map/all_gather | solution.py:39
  1578.2 24.5 %all_gather.51 = bf16[8,16,512]{2,1,0:T(8,128)(2,1)S(1)} all-gather(bf16[1,16,512]{2,1,0:T(8,128)(2,1)S(1)} %slice.1742), channel_id=1, replica_groups=mesh['dp'=8,'chan'=4] {'dp'}, dimensions={0}, use_global_device_ids=true | all-gather | bytes 147456 | tf_op jit(solution)/shard_map/all_gather | solution.py:39
  1618.2 22.3 %psum.202 = bf16[128,96]{0,1:T(8,128)(2,1)S(1)} all-reduce(f32[128,96]{0,1:T(8,128)S(1)} %pad_maximum_fusion.44), channel_id=1, replica_groups=mesh['dp'=8,'chan'=4] {'chan'}, use_global_device_ids=true, to_apply=%region_40.41 | all-reduce | flops 12288 | bytes 73728 | tf_op jit(solution)/shard_map/psum | solution.py:227
  1653.0 15.9 reduce-scatter.11.cloned.1.call-done
  1687.2 59.2 %all-reduce.95.cloned.1.call-done = (f32[1,256]{1,0:T(1,128)}, f32[1,256]{1,0:T(1,128)}, f32[1,4,512]{2,1,0:T(4,128)}, f32[1,4,512]{2,1,0:T(4,128)}, f32[1,512]{...) async-done(((f32[1,256]{1,0:T(1,128)}, f32[1,256]{1,0:T(1,128)}, ...) | async-done | bytes 96272 | tf_op jit(solution)/shard_map/psum | solution.py:342
  1754.3 419.4 %all-reduce.97.cloned.1.call-done = (f32[1,1024,2,512]{3,2,1,0:T(2,128)}, f32[1,1024,2,512]{3,2,1,0:T(2,128)}, f32[1,96,512]{2,1,0:T(8,128)}, f32[1,96,512]{2,1,...) async-done(((f32[1,1024,2,512]{3,2,1,0:T(2,128)}, f32[1,1024,2,512]{3,2,1,0:T(2,128)}, ...) | async-done | bytes 13238288 | tf_op jit(solution)/shard_map/psum | solution.py:342
  (860 shorter events, 867.7 us)
Async XLA Ops:
  7.2 412.7 %reduce-scatter.5.cloned.1.call-start = ((), (), s32[]{:S(2)}) async-start(), calls=%async_computation.4 | async-start | bytes 655360 | tf_op jit(solution)/shard_map/reduce_scatter | solution.py:147
  8.0 418.6 %copy-start.162 = (f32[1,256]{1,0:T(1,128)}, f32[1,256]{1,0:T(1,128)S(1)}, u32[]{:S(2)}) copy-start(f32[1,256]{1,0:T(1,128)S(1)} %get-tuple-element.1051) | copy-start | bytes 3076
  32.3 5.5 collective-permute-start
  37.1 423.7 %copy-start.115 = (f32[16,512]{1,0:T(8,128)}, f32[16,512]{1,0:T(8,128)S(1)}, u32[]{:S(2)}) copy-start(f32[16,512]{1,0:T(8,128)S(1)} %get-tuple-element.1031) | copy-start | bytes 98308
  37.7 347.4 %copy-start.173 = (f32[1,512]{1,0:T(1,128)}, f32[1,512]{1,0:T(1,128)S(1)}, u32[]{:S(2)}) copy-start(f32[1,512]{1,0:T(1,128)S(1)} %get-tuple-element.1046) | copy-start | bytes 6148
  39.5 345.6 %copy-start.44 = (bf16[128,512]{1,0:T(8,128)(2,1)}, bf16[128,512]{1,0:T(8,128)(2,1)S(1)}, u32[]{:S(2)}) copy-start(bf16[128,512]{1,0:T(8,128)(2,1)S(1)} %get-tuple-element.889) | copy-start | bytes 393220
  385.0 49.3 %copy-start.108 = (f32[4,32,512]{2,1,0:T(8,128)}, f32[4,32,512]{2,1,0:T(8,128)S(1)}, u32[]{:S(2)}) copy-start(f32[4,32,512]{2,1,0:T(8,128)S(1)} %multiply_reduce_fusion.11) | copy-start | bytes 786436
  385.1 34.8 %copy-start.72 = (f32[128,256]{1,0:T(8,128)S(1)}, f32[128,256]{1,0:T(8,128)}, u32[]{:S(2)}) copy-start(f32[128,256]{1,0:T(8,128)} %param.30) | copy-start | bytes 393220
  386.4 835.4 %reduce-scatter.9.cloned.1.call-start = ((), (), s32[]{:S(2)}) async-start(), calls=%async_computation.6 | async-start | bytes 327680 | tf_op jit(solution)/shard_map/reduce_scatter | solution.py:262
  386.5 57.4 %copy-start.184 = (f32[128]{0:T(128)S(1)}, f32[128]{0:T(128)}, u32[]{:S(2)}) copy-start(f32[128]{0:T(128)} %copy-done.183) | copy-start | bytes 1540
  386.5 57.4 %copy-start.188 = (f32[128]{0:T(128)S(1)}, f32[128]{0:T(128)}, u32[]{:S(2)}) copy-start(f32[128]{0:T(128)} %copy-done.187) | copy-start | bytes 1540
  386.5 57.4 %copy-start.192 = (f32[128]{0:T(128)S(1)}, f32[128]{0:T(128)}, u32[]{:S(2)}) copy-start(f32[128]{0:T(128)} %copy-done.191) | copy-start | bytes 1540
  386.5 57.4 %copy-start.195 = (f32[1,1,512]{2,1,0:T(1,128)S(1)}, f32[1,1,512]{2,1,0:T(1,128)}, u32[]{:S(2)}) copy-start(f32[1,1,512]{2,1,0:T(1,128)} %get-tuple-element.1037) | copy-start | bytes 6148
  386.5 57.4 %copy-start.197 = (f32[1,1,512]{2,1,0:T(1,128)S(1)}, f32[1,1,512]{2,1,0:T(1,128)}, u32[]{:S(2)}) copy-start(f32[1,1,512]{2,1,0:T(1,128)} %get-tuple-element.1038) | copy-start | bytes 6148
  388.7 58.6 %copy-start.8 = (bf16[128,8,2,512]{3,1,2,0:T(8,128)(2,1)}, bf16[128,8,2,512]{3,1,2,0:T(8,128)(2,1)S(1)}, u32[]{:S(2)}) copy-start(bf16[128,8,2,512]{3,1,2,0:T(8,128)(2,1)S(1)} %copy.71) | copy-start | bytes 6291460
  388.7 32.2 %copy-start.201 = (f32[128]{0:T(128)}, f32[128]{0:T(128)S(1)}, u32[]{:S(2)}) copy-start(f32[128]{0:T(128)S(1)} %convert_element_type.215) | copy-start | bytes 1540
  420.9 42.0 %copy-start.85 = (f32[128,256]{1,0:T(8,128)}, f32[128,256]{1,0:T(8,128)S(1)}, u32[]{:S(2)}) copy-start(f32[128,256]{1,0:T(8,128)S(1)} %get-tuple-element.888) | copy-start | bytes 393220
  434.4 9.4 collective-permute-start.1
  1150.5 40.8 %copy-start.185 = (f32[128]{0:T(128)S(1)}, f32[128]{0:T(128)}, u32[]{:S(2)}) copy-start(f32[128]{0:T(128)} %copy-done.183) | copy-start | bytes 1540
  1150.5 40.8 %copy-start.189 = (f32[128]{0:T(128)S(1)}, f32[128]{0:T(128)}, u32[]{:S(2)}) copy-start(f32[128]{0:T(128)} %copy-done.187) | copy-start | bytes 1540
  1150.5 40.8 %copy-start.193 = (f32[128]{0:T(128)S(1)}, f32[128]{0:T(128)}, u32[]{:S(2)}) copy-start(f32[128]{0:T(128)} %copy-done.191) | copy-start | bytes 1540
  1150.5 40.8 %copy-start.196 = (f32[1,1,512]{2,1,0:T(1,128)S(1)}, f32[1,1,512]{2,1,0:T(1,128)}, u32[]{:S(2)}) copy-start(f32[1,1,512]{2,1,0:T(1,128)} %get-tuple-element.1037) | copy-start | bytes 6148
  1150.5 40.8 %copy-start.198 = (f32[1,1,512]{2,1,0:T(1,128)S(1)}, f32[1,1,512]{2,1,0:T(1,128)}, u32[]{:S(2)}) copy-start(f32[1,1,512]{2,1,0:T(1,128)} %get-tuple-element.1038) | copy-start | bytes 6148
  1150.5 40.8 %copy-start.199 = (f32[1,1,512]{2,1,0:T(1,128)S(1)}, f32[1,1,512]{2,1,0:T(1,128)}, u32[]{:S(2)}) copy-start(f32[1,1,512]{2,1,0:T(1,128)} %get-tuple-element.1043) | copy-start | bytes 6148
  1150.5 40.8 %copy-start.200 = (f32[1,1,512]{2,1,0:T(1,128)S(1)}, f32[1,1,512]{2,1,0:T(1,128)}, u32[]{:S(2)}) copy-start(f32[1,1,512]{2,1,0:T(1,128)} %get-tuple-element.1044) | copy-start | bytes 6148
  1153.0 45.2 %copy-start.9 = (bf16[128,8,2,512]{3,1,2,0:T(8,128)(2,1)S(1)}, bf16[128,8,2,512]{3,1,2,0:T(8,128)(2,1)}, u32[]{:S(2)}) copy-start(bf16[128,8,2,512]{3,1,2,0:T(8,128)(2,1)} %copy-done.8) | copy-start | bytes 6291460
  1193.7 4.4 collective-permute-start.2
  1199.7 42.1 %reduce-scatter.7.cloned.1.call-start = ((), (), s32[]{:S(2)}) async-start(), calls=%async_computation.5 | async-start | bytes 655360 | tf_op jit(solution)/shard_map/reduce_scatter | solution.py:147
  1208.0 460.9 %reduce-scatter.11.cloned.1.call-start = ((), (), s32[]{:S(2)}) async-start(), calls=%async_computation.7 | async-start | bytes 327680 | tf_op jit(solution)/shard_map/reduce_scatter | solution.py:262
  1214.3 27.5 %copy-start.139 = (f32[128,256]{1,0:T(8,128)S(1)}, f32[128,256]{1,0:T(8,128)}, u32[]{:S(2)}) copy-start(f32[128,256]{1,0:T(8,128)} %param.43) | copy-start | bytes 393220
  1214.3 27.5 %copy-start.202 = (f32[128]{0:T(128)S(1)}, f32[128]{0:T(128)}, u32[]{:S(2)}) copy-start(f32[128]{0:T(128)} %copy-done.201) | copy-start | bytes 1540
  1214.3 35.5 %copy-start.45 = (bf16[128,512]{1,0:T(8,128)(2,1)S(1)}, bf16[128,512]{1,0:T(8,128)(2,1)}, u32[]{:S(2)}) copy-start(bf16[128,512]{1,0:T(8,128)(2,1)} %copy-done.44) | copy-start | bytes 393220
  1214.3 35.5 %copy-start.89 = (bf16[2,512,1024]{2,1,0:T(8,128)(2,1)S(1)}, bf16[2,512,1024]{2,1,0:T(8,128)(2,1)}, u32[]{:S(2)}) copy-start(bf16[2,512,1024]{2,1,0:T(8,128)(2,1)} %param.40) | copy-start | bytes 6291460
  1214.3 35.5 %copy-start.97 = (bf16[128,1024]{1,0:T(8,128)(2,1)S(1)}, bf16[128,1024]{1,0:T(8,128)(2,1)}, u32[]{:S(2)}) copy-start(bf16[128,1024]{1,0:T(8,128)(2,1)} %copy-done.95) | copy-start | bytes 786436
  1214.3 35.5 %copy-start.109 = (f32[4,32,512]{2,1,0:T(8,128)S(1)}, f32[4,32,512]{2,1,0:T(8,128)}, u32[]{:S(2)}) copy-start(f32[4,32,512]{2,1,0:T(8,128)} %copy-done.108) | copy-start | bytes 786436
  1214.3 35.5 %copy-start.174 = (f32[1,512]{1,0:T(1,128)S(1)}, f32[1,512]{1,0:T(1,128)}, u32[]{:S(2)}) copy-start(f32[1,512]{1,0:T(1,128)} %copy-done.173) | copy-start | bytes 6148
  1221.8 29.8 %copy-start.37 = (f32[128,512]{1,0:T(8,128)S(1)}, f32[128,512]{1,0:T(8,128)}, u32[]{:S(2)}) copy-start(f32[128,512]{1,0:T(8,128)} %copy-done.36) | copy-start | bytes 786436
  1221.8 29.8 %copy-start.101 = (f32[128,16]{1,0:T(8,128)S(1)}, f32[128,16]{1,0:T(8,128)}, u32[]{:S(2)}) copy-start(f32[128,16]{1,0:T(8,128)} %copy-done.100) | copy-start | bytes 24580
  1221.8 29.8 %copy-start.113 = (f32[16,512]{1,0:T(8,128)S(1)}, f32[16,512]{1,0:T(8,128)}, u32[]{:S(2)}) copy-start(f32[16,512]{1,0:T(8,128)} %copy-done.112) | copy-start | bytes 98308
  1548.2 54.6 %copy-start.92 = (f32[16,512]{1,0:T(8,128)S(1)}, f32[16,512]{1,0:T(8,128)}, u32[]{:S(2)}) copy-start(f32[16,512]{1,0:T(8,128)} %custom-call.3) | copy-start | bytes 98308
  1613.9 26.7 %copy-start.156 = (bf16[2,96,512]{2,1,0:T(8,128)(2,1)S(1)}, bf16[2,96,512]{2,1,0:T(8,128)(2,1)}, u32[]{:S(2)}) copy-start(bf16[2,96,512]{2,1,0:T(8,128)(2,1)} %param.35) | copy-start | bytes 589828
  1642.1 26.8 %copy-start.73 = (f32[128,256]{1,0:T(8,128)S(1)}, f32[128,256]{1,0:T(8,128)}, u32[]{:S(2)}) copy-start(f32[128,256]{1,0:T(8,128)} %param.30) | copy-start | bytes 393220
  1642.1 26.8 %copy-start.161 = (f32[1,256]{1,0:T(1,128)S(1)}, f32[1,256]{1,0:T(1,128)}, u32[]{:S(2)}) copy-start(f32[1,256]{1,0:T(1,128)} %copy-done.160) | copy-start | bytes 3076
  1642.1 26.8 %copy-start.177 = (f32[128]{0:T(128)S(1)}, f32[128]{0:T(128)}, u32[]{:S(2)}) copy-start(f32[128]{0:T(128)} %copy-done.176) | copy-start | bytes 1540
  1642.1 28.5 %copy-start.65 = (bf16[128,1024]{1,0:T(8,128)(2,1)S(1)}, bf16[128,1024]{1,0:T(8,128)(2,1)}, u32[]{:S(2)}) copy-start(bf16[128,1024]{1,0:T(8,128)(2,1)} %copy-done.64) | copy-start | bytes 786436
  1643.1 4.4 collective-permute-start.3
  1649.1 97.3 %all-reduce.95.cloned.1.call-start = ((), (), s32[]{:S(2)}) async-start(), calls=%async_computation.8 | async-start | bytes 192512 | tf_op jit(solution)/shard_map/psum | solution.py:342
  1670.5 503.1 %all-reduce.97.cloned.1.call-start = ((), (), s32[]{:S(2)}) async-start(), calls=%async_computation.9 | async-start | bytes 26476544 | tf_op jit(solution)/shard_map/psum | solution.py:342
  (170 other events, 1448.7 us)
Sparse Core Ops, SparseCore 0:
  386.5 33.2 reduce-scatter.4
  1199.8 17.6 reduce-scatter.8
  1220.0 21.7 reduce-scatter.6
  1649.2 19.6 reduce-scatter.10
  1674.9 71.5 all-reduce.94
  1752.7 420.9 all-reduce.96
where the time goes:
time: 2230 us; the launch traced here: 2190 us
  local copies, waits for them, and re-layouts  893 us (40%)
  waiting for transfers between devices  542 us (24%)
  other arithmetic  371 us (17%)
  blocking collectives  328 us (15%)
  matrix products  31.1 us (1%)
    pad x64, local copies, waits for them, and re-layouts, block_scan(): lax.associative_scan(chain_pair, (dec_blocks, drv_blocks), axis=1)  767 us
    psum x2, waiting for transfers between devices, local(): lax.psum((g_gain, g_in, g_conv_w, g_conv_b, g_x, g_dt, g_bias, g_alog, g_...  479 us
    add x40, other arithmetic, block_scan(): lax.associative_scan(chain_pair, (dec_blocks, drv_blocks), axis=1)  111 us
    all_gather x4, blocking collectives, carried_in(): pieces = jax.tree.map(lambda part: lax.all_gather(part, axis), value)  99 us
    all_gather x4, blocking collectives, prefix(): lax.all_gather(part.astype(kind), axis)  97.5 us
    add x32, other arithmetic, chain_pair(): return (former[0] * latter[0], latter[0] * former[1] + latter[1])  70.1 us
    psum x2, blocking collectives, layer_backward(): grad_proj = lax.psum(back_part, 'chan').astype(jnp.bfloat16)  58.6 us
    dynamic_update_slice x16, other arithmetic, block_scan(): last_pair, joined = lax.scan(link, start, (prod_in, acc_in))  52.6 us
  transfers between devices with their start and end apart: 10, of which 7 were waited for; matrix products, arithmetic and copies ran while one was open for 2% of the time, Pallas kernels for 0%

commit v1 on v0

v1 whole, which is shorter than its diff:
```python
import functools
from types import SimpleNamespace

import jax
import jax.numpy as jnp
from jax import lax
from jax.experimental import pallas as pl
from jax.experimental.pallas import tpu as pltpu
from jax.sharding import PartitionSpec as P

MESH = pl.DeviceIdType.MESH
LANES = 128
ROWS = 8
HALO = 16
EPSILON = 1e-05
RESET = 1e30
F32 = jnp.float32
BF16 = jnp.bfloat16


def dot(left, right, dims=((1,), (0,)), precision=None):
    return lax.dot_general(
        left, right, (dims, ((), ())), precision=precision, preferred_element_type=F32
    )


def silu_slope(value, sig):
    return sig * (1.0 + value * (1.0 - sig))


def wide(column, width):
    return jnp.concatenate([column] * (width // column.shape[1]), axis=1)


def sizes_of(mesh, x_in, in_weight, xproj_weight, dt_weight, a_log, conv_weight):
    z = SimpleNamespace()
    z.ndp = mesh.shape["dp"]
    z.nch = mesh.shape["chan"]
    z.toks, z.quarter = x_in.shape
    z.width = in_weight.shape[1]
    z.chans = in_weight.shape[3]
    z.layers = in_weight.shape[0]
    z.xdim = xproj_weight.shape[1]
    z.rank = dt_weight.shape[1]
    z.states = a_log.shape[1]
    z.taps = conv_weight.shape[1]
    z.half = z.width // 2
    z.total = z.toks * z.ndp
    z.groups = z.chans // LANES
    z.span = 2 * z.groups
    z.pack = -(-(z.xdim + z.rank + z.states + z.taps + 3) // 128) * 128
    z.shared = z.pack % (16 * z.ndp) == 0
    z.piece = z.pack // z.ndp if z.shared else z.pack
    return z


def scratch_of(z):
    t, d, c, n = z.toks, z.width, z.chans, z.ndp
    ext = t + HALO
    vm = pltpu.VMEM
    by_token = [vm((t, c), F32) for _ in range(9)]
    layer = dict(
        hid=vm((ext, d), BF16),
        inv=vm((ext, LANES), F32),
        xs=vm((ext, d), F32),
        inner=vm((ext, c), F32),
        gate=by_token[0],
        slope=by_token[1],
        actf=by_token[2],
        pre=by_token[3],
        step=by_token[4],
        stepk=by_token[5],
        u=by_token[6],
        scan=by_token[7],
        ds=by_token[8],
        act=vm((t, c), BF16),
        gated=vm((t, c), BF16),
        psend=vm((z.xdim, t), BF16),
        pland=vm((z.nch, z.xdim, t), BF16),
        stept=vm((z.rank, t), BF16),
        bce=vm((t, 2 * z.states, LANES), F32),
        dec=vm((t, z.states, c), F32),
        st=vm((t + 1, z.states, c), F32),
        ssend=vm((8, c), F32),
        ssum=vm((n, 8, c), F32),
        carry=vm((2, z.states, c), BF16),
        sland=vm((n, z.states, c), BF16),
        rland=vm((n, z.states, c), BF16),
        bsend=vm((z.xdim, t), BF16),
        bland=vm((z.nch, z.xdim, t), BF16),
        bhalo=vm((z.nch, z.xdim, t), BF16),
        esend=vm((2 * HALO, c), F32),
        eland=vm((2 * HALO, c), F32),
        dm=vm((t, 2 * c), BF16),
        ht=vm((z.quarter, t), BF16),
        gt=vm((c, t), BF16),
        gq=vm((t, d), BF16),
        g=vm((t, d), F32),
        pack=vm((z.pack, c), F32),
        packb=vm((z.pack, c), BF16),
        rsland=vm((n, z.piece, c), BF16),
        small=vm((z.pack, c), BF16),
        gnsend=vm((8, z.quarter), F32),
        gnland=vm((n, 8, z.quarter), F32),
    )
    halves = [vm((t, z.half), BF16) for _ in range(4)]
    reduction = dict(
        a_send=halves[0],
        a_land=halves[1],
        b_send=halves[2],
        b_land=halves[3],
        full=vm((ext, d), F32),
    )
    return dict(
        layers=[dict(layer) for _ in range(z.layers)],
        reductions=[dict(reduction) for _ in range(4)],
        b_halo=vm((2, HALO, z.half), BF16),
        hq=vm((t, z.quarter), BF16),
        cq=vm((t, z.quarter), BF16),
        cot=vm((t, z.quarter), F32),
        meta=vm((16, z.quarter), F32),
        metas=vm((z.nch, 16, z.quarter), F32),
        metah=vm((z.nch, 16, z.quarter), F32),
        gfull=vm((8, d), F32),
        vm=vm((3, ext, LANES), F32),
        dst=vm((t, c), F32),
        adj=vm((t, c), F32),
        dact=vm((t, c), F32),
        dgated=vm((t, c), F32),
        dc=vm((ext, c), F32),
        grow=vm((8, d), F32),
        raw=vm((z.layers, d * z.span, LANES), BF16),
        stage=vm((LANES * z.span, LANES), F32),
        wi=vm((z.layers, d, 2 * c), BF16),
        wo=vm((z.layers, c, d), BF16),
    )


def block_kernel(z, sems, refs):
    v = SimpleNamespace(**refs)
    L = [SimpleNamespace(**one) for one in v.layers]
    R = [SimpleNamespace(**one) for one in v.reductions]
    t, d, c, n = z.toks, z.width, z.chans, z.ndp
    ext = t + HALO
    half, quarter, groups = z.half, z.quarter, z.groups
    rank, ns = z.rank, z.states

    dp = lax.axis_index("dp")
    ch = lax.axis_index("chan")
    bit = lax.rem(ch, 2)
    side = lax.div(ch, 2)
    across = {2: lax.rem(ch + 2, 4)}
    across[1] = ch + 1 - 2 * bit
    across[3] = lax.rem(across[1] + 2, 4)
    pair = lax.rem(dp, 2)
    twin = dp + 1 - 2 * pair
    rank_q = lax.div(dp, 2)
    nq = n // 2
    has_next = dp + 1 < n
    has_prev = dp > 0
    q_cols = pl.ds(pl.multiple_of(ch * quarter, quarter), quarter)
    h_mine = pl.ds(pl.multiple_of(bit * half, half), half)
    h_other = pl.ds(pl.multiple_of((1 - bit) * half, half), half)

    drains = []
    counter = [0]

    def alloc(count):
        base = counter[0]
        counter[0] += count
        return base

    def remote(src, dst, index, target):
        return pltpu.make_async_remote_copy(
            src_ref=src,
            dst_ref=dst,
            send_sem=v.ss.at[index],
            recv_sem=v.rs.at[index],
            device_id=target,
            device_id_type=MESH,
        )

    def send(src, dst, target):
        copy = remote(src, dst, alloc(1), target)
        copy.start()
        drains.append(copy.wait_send)
        return copy

    def chan_send(src, dst):
        return [send(src, dst, (dp, across[p])) for p in (2, 3, 1)]

    def edge_send(pairs, step):
        there, here = (has_next, has_prev) if step > 0 else (has_prev, has_next)
        copies = [
            remote(src, dst, alloc(1), (dp + step, chan)) for src, dst, chan in pairs
        ]

        @pl.when(there)
        def _():
            for copy in copies:
                copy.start()

        def drain():
            @pl.when(there)
            def _():
                for copy in copies:
                    copy.wait_send()

        drains.append(drain)

        def arrive():
            @pl.when(here)
            def _():
                for copy in copies:
                    copy.wait_recv()

        return arrive

    def dp_send(src_of, dst, low, high):
        base = alloc(n)

        def copy_of(o):
            to = lax.rem(dp + o, n)
            return remote(src_of(to), dst, base + o, (to, ch))

        def each(act):
            def body(o, carry):
                act(copy_of(o))
                return carry

            return body

        lax.fori_loop(low, high, each(lambda copy: copy.start()), 0)
        drains.append(
            lambda: lax.fori_loop(low, high, each(lambda copy: copy.wait_send()), 0)
        )

        def arrive(first, last):
            lax.fori_loop(first, last, each(lambda copy: copy.wait_recv()), 0)

        return arrive

    def gather(src, place):
        first, second = alloc(nq), alloc(nq)
        local = pltpu.make_async_copy(src, place(dp), v.ls.at[alloc_local()])
        local.start()

        def hop(o):
            to = lax.rem(rank_q + o, nq) * 2 + pair
            return remote(src, place(dp), first + o, (to, ch))

        def relay(o):
            origin = lax.rem(rank_q - o + nq, nq) * 2 + pair
            return remote(place(origin), place(origin), second + o, (twin, ch))

        own = remote(src, place(dp), second, (twin, ch))

        def start(o, carry):
            hop(o).start()
            return carry

        lax.fori_loop(1, nq, start, 0)
        own.start()

        def forward():
            def body(o, carry):
                hop(o).wait_recv()
                relay(o).start()
                return carry

            lax.fori_loop(1, nq, body, 0)

        def finish():
            def body(o, carry):
                hop(o).wait_send()
                relay(o).wait()
                return carry

            lax.fori_loop(1, nq, body, 0)
            own.wait()
            local.wait()

        return SimpleNamespace(forward=forward, finish=finish)

    locals_used = [2 * z.layers]

    def alloc_local():
        locals_used[0] += 1
        return locals_used[0] - 1

    loads = []
    for l in range(z.layers):
        loads.append(
            (
                pltpu.make_async_copy(
                    v.w_in.at[pl.ds(l * d * z.span, d * z.span), :],
                    v.raw.at[l],
                    v.ls.at[2 * l],
                ),
                pltpu.make_async_copy(v.w_out.at[l], v.wo.at[l], v.ls.at[2 * l + 1]),
            )
        )
        for copy in loads[l]:
            copy.start()

    def load_in(l):
        loads[l][0].wait()
        rows = LANES * z.span

        def body(k, carry):
            at = pl.ds(pl.multiple_of(k * rows, rows), rows)
            to = pl.ds(pl.multiple_of(k * LANES, LANES), LANES)
            v.stage[...] = v.raw[l, at, :].astype(F32)
            for g in range(groups):
                for side_of in range(2):
                    col = side_of * c + g * LANES
                    v.wi[l, to, col : col + LANES] = v.stage[
                        pl.ds(2 * g + side_of, LANES, stride=z.span), :
                    ].astype(BF16)
            return carry

        lax.fori_loop(0, d // LANES, body, 0)

    barrier = pltpu.get_barrier_semaphore()
    for p in (1, 2, 3):
        pl.semaphore_signal(
            barrier, inc=1, device_id=(dp, across[p]), device_id_type=MESH
        )

    def greet(o, carry):
        pl.semaphore_signal(
            barrier, inc=1, device_id=(lax.rem(dp + o, n), ch), device_id_type=MESH
        )
        return carry

    lax.fori_loop(1, n, greet, 0)
    for step in (1, n - 1):
        for p in (1, 2, 3):
            pl.semaphore_signal(
                barrier,
                inc=1,
                device_id=(lax.rem(dp + step, n), across[p]),
                device_id_type=MESH,
            )

    xq = v.x[...]
    v.hq[...] = (xq * v.gain[0:1, :]).astype(BF16)
    v.meta[...] = jnp.zeros_like(v.meta)
    v.meta[0 : z.layers, :] = v.gain[...]
    v.meta[8:16, 0:t] = dot(
        jnp.ones((8, quarter), F32), xq * xq, ((1,), (1,)), lax.Precision.HIGHEST
    )
    mask = jnp.broadcast_to(v.mask[...].astype(F32), (8, t))
    cot = v.probe[...] * jnp.transpose(mask)[:, 0:1]
    v.cot[...] = cot
    v.cq[...] = cot.astype(BF16)

    @pl.when(jnp.logical_not(has_prev))
    def _():
        L[0].hid[0:HALO, :] = jnp.zeros((HALO, d), BF16)
        L[0].xs[0:HALO, :] = jnp.zeros((HALO, d), F32)
        v.metah[...] = jnp.zeros_like(v.metah)
        v.b_halo[...] = jnp.zeros_like(v.b_halo)

    @pl.when(jnp.logical_not(has_next))
    def _():
        for l in range(z.layers):
            L[l].bhalo[...] = jnp.zeros_like(L[l].bhalo)
            L[l].eland[...] = jnp.zeros_like(L[l].eland)

    pl.semaphore_wait(barrier, 3 + (n - 1) + 6)

    own = pl.ds(HALO, t)
    head = pl.ds(0, HALO)
    tail = pl.ds(t - HALO, HALO)
    everyone = [ch, across[1], across[2], across[3]]
    got_h = chan_send(v.hq, L[0].hid.at[own, q_cols])
    got_m = chan_send(v.meta, v.metas.at[ch])
    got_edge = edge_send(
        [(v.hq.at[tail, :], L[0].hid.at[head, q_cols], k) for k in everyone]
        + [(v.meta, v.metah.at[ch], k) for k in everyone],
        1,
    )
    got_x = chan_send(v.x, L[0].xs.at[own, q_cols])
    got_xedge = edge_send(
        [(v.x.at[tail, :], L[0].xs.at[head, q_cols], k) for k in everyone], 1
    )
    got_c = chan_send(v.cq, L[1].gq.at[:, q_cols])
    got_g = chan_send(v.cot, L[1].g.at[:, q_cols])
    L[0].hid[own, q_cols] = v.hq[...]
    v.metas[ch] = v.meta[...]
    L[0].xs[own, q_cols] = xq
    L[1].gq[:, q_cols] = v.cq[...]
    L[1].g[:, q_cols] = cot

    position = dp * t + lax.broadcasted_iota(jnp.int32, (ext, LANES), 0)
    first = jnp.zeros((ext, LANES), jnp.int32)
    start = jnp.int32(0)
    for s in range(v.lengths.shape[0]):
        first = jnp.where(position >= start, start, first)
        start = start + v.lengths[s]
    offset = position - first
    for k in range(z.taps - 1):
        v.vm[k] = jnp.where(offset >= z.taps - 1 - k, 1.0, 0.0).astype(F32)

    def valid(k, rows, width):
        return wide(v.vm[k, rows, :], width)

    def a_of(l):
        return -jnp.exp(v.a_log[l])

    def lane(g):
        return slice(g * LANES, (g + 1) * LANES)

    def fwd_head(l):
        hid, inv = L[l].hid, L[l].inv
        scale = wide(inv[...], c)
        mixed = dot(hid[...], v.wi[l, :, 0:c])
        inner = (scale * mixed).astype(BF16).astype(F32)
        L[l].inner[...] = inner
        conv = jnp.broadcast_to(v.conv_b[l : l + 1, :], (t, c))
        for k in range(z.taps):
            at = HALO - z.taps + 1 + k
            term = v.conv_w[l, k : k + 1, :] * L[l].inner[at : at + t, :]
            conv = conv + (term if k == z.taps - 1 else term * valid(k, slice(0, t), c))
        sig = jax.nn.sigmoid(conv)
        act = (conv * sig).astype(BF16)
        L[l].act[...] = act
        L[l].actf[...] = act.astype(F32)
        part = dot(v.w_x[l], act, ((1,), (1,))).astype(BF16)
        L[l].psend[...] = part
        got = chan_send(L[l].psend, L[l].pland.at[ch])
        L[l].pland[ch] = part
        L[l].slope[...] = silu_slope(conv, sig)
        gate = dot(hid[own, :], v.wi[l, :, c : 2 * c])
        L[l].gate[...] = (wide(inv[own, :], c) * gate).astype(BF16).astype(F32)
        return got

    def fwd_mid(l, got):
        for copy in got:
            copy.wait_recv()
        land = L[l].pland
        proj = land[0].astype(F32)
        for k in range(1, z.nch):
            proj = proj + land[k].astype(F32)
        stept = proj[0:rank, :].astype(BF16)
        L[l].stept[...] = stept
        pre = dot(stept, v.w_dt[l], ((0,), (0,))) + v.dt_b[l : l + 1, :]
        step = jnp.maximum(pre, 0.0) + jnp.log1p(jnp.exp(-jnp.abs(pre)))
        stepk = step + (1.0 - valid(z.taps - 2, slice(0, t), c)) * RESET
        L[l].pre[...] = pre
        L[l].step[...] = step
        L[l].stepk[...] = stepk
        L[l].u[...] = step * L[l].actf[...]
        L[l].ssend[...] = jnp.broadcast_to(
            jnp.sum(stepk, axis=0, keepdims=True), (8, c)
        )
        got_s = dp_send(lambda to: L[l].ssend, L[l].ssum.at[dp], 1, n)
        bc = proj[rank : rank + 2 * ns, :]
        lanes = lax.broadcasted_iota(jnp.int32, (2 * ns, t), 1)
        bce = L[l].bce

        def spread(block, carry):
            for i in range(ROWS):
                tok = block * ROWS + i
                column = jnp.sum(
                    jnp.where(lanes == tok, bc, 0.0), axis=1, keepdims=True
                )
                bce[tok] = jnp.broadcast_to(column, (2 * ns, LANES))
            return carry

        lax.fori_loop(0, t // ROWS, spread, 0)
        return got_s

    def scan_sum(l):
        a = a_of(l)
        stepk, u, bce, dec = L[l].stepk, L[l].u, L[l].bce, L[l].dec

        def body(block, state):
            state = list(state)
            rows = pl.ds(pl.multiple_of(block * ROWS, ROWS), ROWS)
            sk, uu = stepk[rows, :], u[rows, :]
            for i in range(ROWS):
                tok = block * ROWS + i
                b = bce[tok, 0:ns, :]
                for g in range(groups):
                    e = jnp.exp(sk[i : i + 1, lane(g)] * a[:, lane(g)])
                    dec[tok, :, lane(g)] = e
                    state[g] = e * state[g] + uu[i : i + 1, lane(g)] * b
            return tuple(state)

        zero = jnp.zeros((ns, LANES), F32)
        return lax.fori_loop(0, t // ROWS, body, (zero,) * groups)

    def back_sum(l):
        ds, bce, dec = L[l].ds, L[l].bce, L[l].dec

        def body(k, flow):
            flow = list(flow)
            block = t // ROWS - 1 - k
            rows = pl.ds(pl.multiple_of(block * ROWS, ROWS), ROWS)
            dd = ds[rows, :]
            for i in reversed(range(ROWS)):
                tok = block * ROWS + i
                cc = bce[tok, ns : 2 * ns, :]
                for g in range(groups):
                    lam = cc * dd[i : i + 1, lane(g)] + flow[g]
                    flow[g] = dec[tok, :, lane(g)] * lam
            return tuple(flow)

        zero = jnp.zeros((ns, LANES), F32)
        return lax.fori_loop(0, t // ROWS, body, (zero,) * groups)

    def put(ref, k, parts):
        for g in range(groups):
            ref[k, :, lane(g)] = parts[g].astype(BF16)

    def carry_in(l, land, order, count):
        a = a_of(l)

        def body(k, carry):
            j = order(k)
            return (
                jnp.exp(a * L[l].ssum[j, 0:1, :]) * carry + land[j].astype(F32)
            )

        return lax.fori_loop(0, count, body, jnp.zeros((ns, c), F32))

    def scan_out(l, carry):
        u, bce, dec, st = L[l].u, L[l].bce, L[l].dec, L[l].st
        y = L[l].scan
        st[0] = carry

        def body(block, state):
            state = list(state)
            rows = pl.ds(pl.multiple_of(block * ROWS, ROWS), ROWS)
            uu = u[rows, :]
            outs = [[] for _ in range(groups)]
            for i in range(ROWS):
                tok = block * ROWS + i
                b = bce[tok, 0:ns, :]
                cc = bce[tok, ns : 2 * ns, :]
                for g in range(groups):
                    s = dec[tok, :, lane(g)] * state[g] + uu[i : i + 1, lane(g)] * b
                    st[tok + 1, :, lane(g)] = s
                    state[g] = s
                    outs[g].append(jnp.sum(cc * s, axis=0, keepdims=True))
            for g in range(groups):
                y[rows, lane(g)] = jnp.concatenate(outs[g], axis=0)
            return tuple(state)

        lax.fori_loop(
            0, t // ROWS, body, tuple(carry[:, lane(g)] for g in range(groups))
        )
        scanned = y[...] + v.skip[l : l + 1, :] * L[l].actf[...]
        y[...] = scanned
        gate = L[l].gate[...]
        gated = (scanned * gate * jax.nn.sigmoid(gate)).astype(BF16)
        L[l].gated[...] = gated
        return gated

    def reduce_a(k, part_of):
        send_ref, keep_ref = R[k].a_send, R[k].full
        send_ref[...] = part_of(h_other).astype(BF16)
        got = send(send_ref, R[k].a_land, (dp, across[1]))
        keep_ref[own, h_mine] = part_of(h_mine)
        return got

    def reduce_b(k, got, edge):
        got.wait_recv()
        b_send = R[k].b_send
        b_send[...] = (
            R[k].full[own, h_mine]
            + R[k].a_land[...].astype(F32)
        ).astype(BF16)
        got = send(b_send, R[k].b_land, (dp, across[2]))
        arrive = None
        if edge:
            arrive = edge_send(
                [
                    (b_send.at[tail, :], v.b_halo.at[side], chan)
                    for chan in (ch, across[2])
                ],
                1,
            )
        return got, arrive

    def reduce_c(k, got, arrive):
        got.wait_recv()
        full = R[k].full
        full[own, h_mine] = R[k].b_send[...].astype(F32) + R[k].b_land[...].astype(F32)
        region = full.at[own, h_mine]
        if arrive is not None:
            arrive()
            full[head, h_mine] = v.b_halo[0].astype(F32) + v.b_halo[1].astype(F32)
            region = full.at[:, h_mine]
        return send(region, region, (dp, across[1]))

    def reduce_all(k, part_of, edge=False):
        a = reduce_a(k, part_of)
        b, arrive = reduce_b(k, a, edge)
        reduce_c(k, b, arrive).wait_recv()

    def out_part(l):
        return lambda cols: dot(L[l].gated[...], v.wo[l, :, cols])

    def in_part(l):
        return lambda cols: dot(L[l].dm[...], v.wi[l, cols, :], ((1,), (1,)))

    def back_gate(l):
        dgated = dot(L[l].gq[...], v.wo[l], ((1,), (1,)))
        gate = L[l].gate[...]
        v.dgated[...] = dgated
        L[l].ds[...] = dgated * gate * jax.nn.sigmoid(gate)

    def back_dgate(l):
        gate = L[l].gate[...]
        sig = jax.nn.sigmoid(gate)
        dgate = v.dgated[...] * L[l].scan[...] * silu_slope(gate, sig)
        L[l].dm[:, c : 2 * c] = (wide(L[l].inv[own, :], c) * dgate).astype(
            BF16
        )

    def back_scan(l, flow_in):
        a = a_of(l)
        ds, u, bce, dec, st = L[l].ds, L[l].u, L[l].bce, L[l].dec, L[l].st
        stepk, actf = L[l].stepk, L[l].actf
        lanes = lax.broadcasted_iota(jnp.int32, (ns, t), 1)

        def body(k, carry):
            flow, acc, acc_b, acc_c = list(carry[0]), list(carry[1]), carry[2], carry[3]
            block = t // ROWS - 1 - k
            rows = pl.ds(pl.multiple_of(block * ROWS, ROWS), ROWS)
            dd, uu, sk, aa = ds[rows, :], u[rows, :], stepk[rows, :], actf[rows, :]
            d_step = [[] for _ in range(groups)]
            d_adj = [[] for _ in range(groups)]
            for i in reversed(range(ROWS)):
                tok = block * ROWS + i
                b = bce[tok, 0:ns, :]
                cc = bce[tok, ns : 2 * ns, :]
                sum_b = jnp.zeros((ns, LANES), F32)
                sum_c = jnp.zeros((ns, LANES), F32)
                for g in range(groups):
                    drow = dd[i : i + 1, lane(g)]
                    lam = cc * drow + flow[g]
                    flow[g] = dec[tok, :, lane(g)] * lam
                    rate = flow[g] * st[tok, :, lane(g)]
                    acc[g] = acc[g] + rate * sk[i : i + 1, lane(g)]
                    adj = jnp.sum(lam * b, axis=0, keepdims=True)
                    d_adj[g].insert(0, adj)
                    d_step[g].insert(
                        0,
                        jnp.sum(rate * a[:, lane(g)], axis=0, keepdims=True)
                        + adj * aa[i : i + 1, lane(g)],
                    )
                    sum_b = sum_b + lam * uu[i : i + 1, lane(g)]
                    sum_c = sum_c + st[tok + 1, :, lane(g)] * drow
                acc_b = jnp.where(
                    lanes == tok, jnp.sum(sum_b, axis=1, keepdims=True), acc_b
                )
                acc_c = jnp.where(
                    lanes == tok, jnp.sum(sum_c, axis=1, keepdims=True), acc_c
                )
            for g in range(groups):
                v.dst[rows, lane(g)] = jnp.concatenate(d_step[g], axis=0)
                v.adj[rows, lane(g)] = jnp.concatenate(d_adj[g], axis=0)
            return (tuple(flow), tuple(acc), acc_b, acc_c)

        zero = jnp.zeros((ns, LANES), F32)
        _, acc, acc_b, acc_c = lax.fori_loop(
            0,
            t // ROWS,
            body,
            (
                tuple(flow_in[:, lane(g)] for g in range(groups)),
                (zero,) * groups,
                jnp.zeros((ns, t), F32),
                jnp.zeros((ns, t), F32),
            ),
        )
        at = z.xdim + rank
        for g in range(groups):
            L[l].pack[at : at + ns, lane(g)] = acc[g] * a[:, lane(g)]
        return acc_b, acc_c

    def back_mid(l, acc_b, acc_c):
        pack = L[l].pack
        actf = L[l].actf[...]
        ds = L[l].ds[...]
        dpre = v.dst[...] * jax.nn.sigmoid(L[l].pre[...])
        dpre_q = dpre.astype(BF16)
        bsend = L[l].bsend
        bsend[0:rank, :] = dot(v.w_dt[l], dpre_q, ((1,), (1,))).astype(BF16)
        bsend[rank : rank + ns, :] = acc_b.astype(BF16)
        bsend[rank + ns : rank + 2 * ns, :] = acc_c.astype(BF16)
        got = chan_send(bsend, L[l].bland.at[ch])
        L[l].bland[ch] = bsend[...]
        dact = ds * v.skip[l : l + 1, :] + L[l].step[...] * v.adj[...]
        v.dact[...] = dact
        L[l].esend[0:HALO, :] = dact[0:HALO, :]
        L[l].esend[HALO : 2 * HALO, :] = L[l].slope[0:HALO, :]
        edge = edge_send(
            [(L[l].esend, L[l].eland, ch)]
            + [(bsend, L[l].bhalo.at[ch], k) for k in everyone],
            -1,
        )
        pack[z.xdim : z.xdim + rank, :] = dot(L[l].stept[...], dpre_q)
        at = z.xdim + rank + ns + z.taps
        pack[at + 1 : at + 2, :] = jnp.sum(dpre, axis=0, keepdims=True)
        pack[at + 2 : at + 3, :] = jnp.sum(ds * actf, axis=0, keepdims=True)
        if at + 3 < z.pack:
            pack[at + 3 :, :] = jnp.zeros((z.pack - at - 3, c), F32)
        return got, edge

    def sum_land(ref):
        total = ref[0].astype(F32)
        for k in range(1, z.nch):
            total = total + ref[k].astype(F32)
        return total.astype(BF16)

    def back_conv(l, got, edge):
        pack = L[l].pack
        for copy in got:
            copy.wait_recv()
        edge()
        dproj = sum_land(L[l].bland)
        dproj_h = sum_land(L[l].bhalo)
        wx = v.w_x[l]
        dact = v.dact[...] + dot(dproj, wx, ((0,), (0,)))
        dconv = dact * L[l].slope[...]
        v.dc[0:t, :] = dconv
        eland = L[l].eland
        after = dot(dproj_h, wx, ((0,), (0,)))[0:HALO, :]
        v.dc[t:ext, :] = (eland[0:HALO, :] + after) * eland[HALO : 2 * HALO, :]
        dinner = jnp.zeros((t, c), F32)
        for k in range(z.taps):
            at = z.taps - 1 - k
            rows = slice(at, at + t)
            term = v.dc[rows, :] * v.conv_w[l, k : k + 1, :]
            dinner = dinner + (
                term if k == z.taps - 1 else term * valid(k, rows, c)
            )
        L[l].dm[:, 0:c] = (wide(L[l].inv[own, :], c) * dinner).astype(BF16)
        return dproj

    def back_rest(l, dproj):
        pack = L[l].pack
        pack[0 : z.xdim, :] = dot(dproj, L[l].act[...])
        dconv = v.dc[0:t, :]
        at = z.xdim + rank + ns
        for k in range(z.taps):
            row = HALO - z.taps + 1 + k
            term = dconv * L[l].inner[row : row + t, :]
            if k < z.taps - 1:
                term = term * valid(k, slice(0, t), c)
            pack[at + k : at + k + 1, :] = jnp.sum(term, axis=0, keepdims=True)
        pack[at + z.taps : at + z.taps + 1, :] = jnp.sum(dconv, axis=0, keepdims=True)

    def back_norm(l, k):
        u = R[k].full[own, :]
        x = L[l].xs[own, :]
        scaled = u * v.gfull[l : l + 1, :]
        xhat = x * wide(L[l].inv[own, :], d)
        mean = jnp.sum(scaled * xhat, axis=1, keepdims=True) * (1.0 / d)
        v.grow[...] = jnp.broadcast_to(jnp.sum(u * x, axis=0, keepdims=True), (8, d))
        L[l].gnsend[...] = v.grow[:, q_cols]
        L[l].gnland[dp] = v.grow[:, q_cols]
        arrive = dp_send(
            lambda to: L[l].gnsend, L[l].gnland.at[dp], 1, n
        )
        return L[l].g[...] + scaled - xhat * mean, arrive

    def gain_out(l, arrive):
        arrive(1, n)
        total = lax.fori_loop(
            0, n, lambda j, s: s + L[l].gnland[j], jnp.zeros((8, quarter), F32)
        )
        v.gains[l : l + 1, :] = total[0:1, :]

    def small_scatter(l):
        if not z.shared:
            v.smalls[l] = L[l].pack[...]
            return None
        rows = z.piece
        packb = L[l].packb
        packb[...] = L[l].pack[...].astype(BF16)
        piece = lambda j: pl.ds(pl.multiple_of(j * rows, rows), rows)
        arrive = dp_send(
            lambda to: packb.at[piece(to), :], L[l].rsland.at[dp], 1, n
        )
        L[l].rsland[dp] = packb[piece(dp), :]
        return arrive

    def small_gather(l, arrive):
        if not z.shared:
            return None
        rows = z.piece
        arrive(1, n)
        total = lax.fori_loop(
            0,
            n,
            lambda j, s: s + L[l].rsland[j].astype(F32),
            jnp.zeros((rows, c), F32),
        )
        mine = pl.ds(pl.multiple_of(dp * rows, rows), rows)
        L[l].small[mine, :] = total.astype(BF16)
        return dp_send(
            lambda to: L[l].small.at[mine, :], L[l].small.at[mine, :], 1, n
        )

    def small_out(l, arrive):
        if z.shared:
            arrive(1, n)
            v.smalls[l] = L[l].small[...]

    def inverse(total):
        return lax.rsqrt(total * (1.0 / d) + EPSILON)

    def norms():
        sums, sums_h = v.metas[0, 8:16, 0:t], v.metah[0, 8:16, 0:t]
        v.gfull[:, 0:quarter] = v.metas[0, 0:8, :]
        for k in range(1, z.nch):
            sums = sums + v.metas[k, 8:16, 0:t]
            sums_h = sums_h + v.metah[k, 8:16, 0:t]
            v.gfull[:, k * quarter : (k + 1) * quarter] = v.metas[k, 0:8, :]
        L[0].inv[own, :] = jnp.broadcast_to(
            jnp.transpose(inverse(sums))[:, 0:1], (t, LANES)
        )
        L[0].inv[head, :] = jnp.broadcast_to(
            jnp.transpose(inverse(sums_h))[t - HALO : t, 0:1], (HALO, LANES)
        )

    def lanes_at(l, ref, rows):
        return lambda j: ref.at[l, rows, pl.ds(pl.multiple_of(j * t, t), t)]

    def rows_at(l, ref, cols, low=0, high=t):
        return lambda j: ref.at[
            l, pl.ds(pl.multiple_of(j * t + low, high - low), high - low), cols
        ]

    def gather_hid(l):
        L[l].ht[...] = jnp.transpose(L[l].hid[own, q_cols])
        return gather(L[l].ht, lanes_at(l, v.hid_all, q_cols))

    def gather_gat(l):
        L[l].gt[...] = jnp.transpose(L[l].gated[...])
        return gather(L[l].gt, lanes_at(l, v.gat_all, slice(None)))

    def gather_gq(l):
        return gather(L[l].gq.at[:, q_cols], rows_at(l, v.gq_all, q_cols))

    def gather_dmg(l):
        cols = slice(c, 2 * c)
        return gather(L[l].dm.at[:, cols], rows_at(l, v.dmg_all, slice(None)))

    def gather_dmi(l, low=0, high=t):
        src = L[l].dm.at[low:high, 0:c]
        return gather(src, rows_at(l, v.dmi_all, slice(None), low, high))

    def quarter_at(k):
        return pl.ds(pl.multiple_of(k * quarter, quarter), quarter)

    def share(region):
        mine = region(ch)
        got = send(mine, mine, (dp, across[2]))

        def second():
            got.wait_recv()
            theirs = region(across[2])
            one = send(mine, mine, (dp, across[1]))
            two = send(theirs, theirs, (dp, across[1]))

            def done():
                one.wait_recv()
                two.wait_recv()

            return done

        return second

    def share_hid(l):
        return share(lambda k: v.hid_all.at[l, quarter_at(k), :])

    def share_gq(l):
        return share(lambda k: v.gq_all.at[l, :, quarter_at(k)])

    hid0 = gather_hid(0)
    gq1 = gather_gq(1)
    load_in(0)
    for copy in got_h + got_m:
        copy.wait_recv()
    got_edge()
    norms()
    got_p = fwd_head(0)
    load_in(1)
    got_s0 = fwd_mid(0, got_p)
    put(L[0].carry, 0, scan_sum(0))
    got_carry = dp_send(lambda to: L[0].carry.at[0], L[0].sland.at[dp], 1, n - dp)
    for copy in got_x + got_c + got_g:
        copy.wait_recv()
    got_xedge()
    loads[0][1].wait()
    got_s0(1, n)
    got_carry(1, dp + 1)
    hid0.forward()
    gq1.forward()
    scan_out(0, carry_in(0, L[0].sland, lambda k: k, dp))
    red0 = reduce_a(0, out_part(0))
    gat0 = gather_gat(0)
    red0, arrive = reduce_b(0, red0, True)
    reduce_c(0, red0, arrive).wait_recv()
    x1 = L[0].xs[...] + R[0].full[...]
    L[1].xs[...] = x1
    L[1].hid[...] = (x1 * v.gfull[1:2, :]).astype(BF16)
    L[1].inv[...] = jnp.broadcast_to(
        inverse(jnp.sum(x1 * x1, axis=1, keepdims=True)), (ext, LANES)
    )

    got_p = fwd_head(1)
    hid1 = gather_hid(1)
    gat0.forward()
    loads[1][1].wait()
    back_gate(1)
    got_s1 = fwd_mid(1, got_p)
    hid0.finish()
    share0 = share_hid(0)
    put(L[1].carry, 0, scan_sum(1))
    put(L[1].carry, 1, back_sum(1))
    got_f = dp_send(lambda to: L[1].carry.at[0], L[1].sland.at[dp], 1, n - dp)
    got_r = dp_send(lambda to: L[1].carry.at[1], L[1].rland.at[dp], n - dp, n)
    got_s1(1, n)
    got_f(1, dp + 1)
    got_r(dp + 1, n)
    hid1.forward()
    gq1.finish()
    share1 = share_gq(1)
    scan_out(1, carry_in(1, L[1].sland, lambda k: k, dp))
    gat1 = gather_gat(1)
    back_dgate(1)
    dmg1 = gather_dmg(1)
    red1 = reduce_a(1, out_part(1))

    acc_b, acc_c = back_scan(1, carry_in(1, L[1].rland, lambda k: n - 1 - k, n - 1 - dp))
    got_b, edge = back_mid(1, acc_b, acc_c)
    share0 = share0()
    red1, _ = reduce_b(1, red1, False)
    gat1.forward()
    dproj = back_conv(1, got_b, edge)
    red2 = reduce_a(2, in_part(1))
    dmg1.forward()
    dmi1 = gather_dmi(1)
    back_rest(1, dproj)
    red2, _ = reduce_b(2, red2, False)
    share1 = share1()
    reduce_c(1, red1, None).wait_recv()
    v.block_out[...] = L[1].xs[own, q_cols] + R[1].full[own, q_cols]
    reduce_c(2, red2, None).wait_recv()
    grad, gain1 = back_norm(1, 2)
    L[0].g[...] = grad
    L[0].gq[...] = grad.astype(BF16)

    back_gate(0)
    put(L[0].carry, 1, back_sum(0))
    got_r = dp_send(lambda to: L[0].carry.at[1], L[0].rland.at[dp], n - dp, n)
    gq0 = gather_gq(0)
    back_dgate(0)
    hid1.finish()
    share2 = share_hid(1)
    got_r(dp + 1, n)
    dmg0 = gather_dmg(0)
    dmi1.forward()
    small1 = small_scatter(1)
    acc_b, acc_c = back_scan(0, carry_in(0, L[0].rland, lambda k: n - 1 - k, n - 1 - dp))
    got_b, edge = back_mid(0, acc_b, acc_c)
    share2 = share2()
    gq0.forward()
    dproj = back_conv(0, got_b, edge)
    dmi0 = [gather_dmi(0, 0, t // 2), gather_dmi(0, t // 2, t)]
    red3 = reduce_a(3, in_part(0))
    dmg0.forward()
    back_rest(0, dproj)
    small0 = small_scatter(0)
    small1 = small_gather(1, small1)
    red3, _ = reduce_b(3, red3, False)
    gq0.finish()
    dmi0[0].forward()
    reduce_c(3, red3, None).wait_recv()
    share3 = share_gq(0)
    grad, gain0 = back_norm(0, 3)
    L[0].g[...] = grad
    v.input_grad[...] = L[0].g[:, q_cols]
    dmi0[1].forward()
    small0 = small_gather(0, small0)
    share3 = share3()
    gain_out(0, gain0)
    gain_out(1, gain1)
    small_out(1, small1)
    small_out(0, small0)
    for one in (share0, share1, share2, share3):
        one()
    for one in (gat0, gat1, dmg1, dmi1, dmg0, *dmi0):
        one.finish()
    for drain in drains:
        drain()
    assert counter[0] <= sems[0] and locals_used[0] <= sems[1], (counter, locals_used)


def run_blocks(z, args):
    sems = (160 + 11 * 2 * (z.ndp // 2) + 13 * z.ndp, 4 + 11)
    vmem = pl.BlockSpec(memory_space=pltpu.VMEM)
    smem = pl.BlockSpec(memory_space=pltpu.SMEM)
    anywhere = pl.BlockSpec(memory_space=pl.ANY)
    specs = dict.fromkeys(args, vmem) | dict(
        lengths=smem, w_in=anywhere, w_out=anywhere
    )
    t, d, c, n, layers = z.toks, z.width, z.chans, z.total, z.layers
    shape = jax.ShapeDtypeStruct
    outs = dict(
        block_out=(shape((t, z.quarter), F32), vmem),
        input_grad=(shape((t, z.quarter), F32), vmem),
        smalls=(shape((layers, z.pack, c), BF16 if z.shared else F32), vmem),
        gains=(shape((layers, z.quarter), F32), vmem),
        hid_all=(shape((layers, d, n), BF16), anywhere),
        gat_all=(shape((layers, c, n), BF16), anywhere),
        gq_all=(shape((layers, n, d), BF16), anywhere),
        dmi_all=(shape((layers, n, c), BF16), anywhere),
        dmg_all=(shape((layers, n, c), BF16), anywhere),
    )
    scratch = scratch_of(z)
    flags = dict(
        ss=pltpu.SemaphoreType.DMA((sems[0],)),
        rs=pltpu.SemaphoreType.DMA((sems[0],)),
        ls=pltpu.SemaphoreType.DMA((sems[1],)),
    )
    parts = [args, outs, scratch, flags]
    leaf = lambda node: not isinstance(node, (dict, list))
    trees = [jax.tree.flatten(part, is_leaf=leaf) for part in parts]
    whole = jax.tree.structure([dict(part) for part in parts], is_leaf=leaf)

    def kernel(*refs):
        merged = {}
        for part in jax.tree.unflatten(whole, refs):
            merged |= part
        block_kernel(z, sems, merged)

    results = pl.pallas_call(
        kernel,
        out_shape=[one[0] for one in trees[1][0]],
        in_specs=jax.tree.leaves(specs, is_leaf=leaf),
        out_specs=[one[1] for one in trees[1][0]],
        scratch_shapes=trees[2][0] + trees[3][0],
        compiler_params=pltpu.CompilerParams(
            collective_id=0, has_side_effects=True, vmem_limit_bytes=62 * 2**20
        ),
        name="blocks",
    )(*trees[0][0])
    return SimpleNamespace(**jax.tree.unflatten(trees[1][1], results))


def grad_kernel(z, steps, hid, gat, gq, dmi, dmg, smalls, small_ins, win, wout, *outs):
    rows = hid.shape[1]
    first = pl.program_id(2) == 0
    lhs = hid[0]
    groups = z.groups
    for k, rhs in enumerate((dmi, dmg)):
        part = dot(lhs, rhs[0])
        for j in range(groups):
            at = pl.ds(j * 2 + k, rows, stride=z.span)
            piece = part[:, j * LANES : (j + 1) * LANES]
            if steps == 1:
                win[at, :] = piece
            else:
                win[at, :] = jnp.where(first, 0.0, win[at, :]) + piece
    part = dot(gat[0], gq[0])
    if steps == 1:
        wout[0] = part
    else:
        wout[0] = jnp.where(first, 0.0, wout[0]) + part

    begin = first & (pl.program_id(0) == 0) & (pl.program_id(1) == 0)

    @pl.when(begin)
    def _():
        for src, to in zip(small_ins, outs[:3], strict=True):
            to[...] = src[...]
        at = 0
        for to in outs[3:]:
            for l in range(z.layers):
                if len(to.shape) == 3:
                    count = to.shape[1]
                    to[l] = smalls[l, at : at + count, :].astype(F32)
                else:
                    count = 1
                    to[l : l + 1, :] = smalls[l, at : at + 1, :].astype(F32)
            at += count


def weight_grads(z, r):
    blocks = 4
    deep = min(z.total, 1024)
    steps = z.total // deep
    layers, d, c = z.layers, z.width, z.chans
    rows, orow = d // blocks, c // blocks
    shape = jax.ShapeDtypeStruct
    small_shapes = (
        r.block_out,
        r.input_grad,
        r.gains,
        shape((layers, z.xdim, c), F32),
        shape((layers, z.rank, c), F32),
        shape((layers, z.states, c), F32),
        shape((layers, z.taps, c), F32),
        shape((layers, c), F32),
        shape((layers, c), F32),
        shape((layers, c), F32),
    )

    def fixed(one):
        dims = len(one.shape)
        return pl.BlockSpec(one.shape, lambda l, i, k: (0,) * dims)

    def kernel(hid, gat, gq, dmi, dmg, smalls, block_out, input_grad, gains, *outs):
        ins = (block_out, input_grad, gains)
        grad_kernel(z, steps, hid, gat, gq, dmi, dmg, smalls, ins, *outs)

    win, wout, *rest = pl.pallas_call(
        kernel,
        grid=(layers, blocks, steps),
        out_shape=[
            shape((layers * d * z.span, LANES), F32),
            shape((layers, c, d), F32),
            *[shape(one.shape, F32) for one in small_shapes],
        ],
        in_specs=[
            pl.BlockSpec((1, rows, deep), lambda l, i, k: (l, i, k)),
            pl.BlockSpec((1, orow, deep), lambda l, i, k: (l, i, k)),
            pl.BlockSpec((1, deep, d), lambda l, i, k: (l, k, 0)),
            pl.BlockSpec((1, deep, c), lambda l, i, k: (l, k, 0)),
            pl.BlockSpec((1, deep, c), lambda l, i, k: (l, k, 0)),
            fixed(r.smalls),
            fixed(r.block_out),
            fixed(r.input_grad),
            fixed(r.gains),
        ],
        out_specs=[
            pl.BlockSpec((rows * z.span, LANES), lambda l, i, k: (l * blocks + i, 0)),
            pl.BlockSpec((1, orow, d), lambda l, i, k: (l, i, 0)),
            *[fixed(one) for one in small_shapes],
        ],
        compiler_params=pltpu.CompilerParams(vmem_limit_bytes=56 * 2**20),
        name="weight_grads",
    )(
        r.hid_all,
        r.gat_all,
        r.gq_all,
        r.dmi_all,
        r.dmg_all,
        r.smalls,
        r.block_out,
        r.input_grad,
        r.gains,
    )
    win = win.reshape(layers, d, z.groups, 2, LANES).transpose(0, 1, 3, 2, 4)
    return win.reshape(layers, d, 2, c), wout, rest


def local(
    mesh,
    x_in,
    norm_gain,
    in_weight,
    conv_weight,
    conv_bias,
    xproj_weight,
    dt_weight,
    dt_bias,
    a_log,
    skip_gain,
    out_weight,
    seq_lengths,
    char_mask,
    out_probe,
):
    z = sizes_of(mesh, x_in, in_weight, xproj_weight, dt_weight, a_log, conv_weight)
    w_in = in_weight.reshape(z.layers, z.width, 2, z.groups, LANES)
    w_in = w_in.transpose(0, 1, 3, 2, 4).reshape(-1, LANES)
    r = run_blocks(
        z,
        dict(
            lengths=seq_lengths,
            x=x_in,
            gain=norm_gain,
            probe=out_probe,
            mask=char_mask.reshape(1, z.toks),
            w_in=w_in,
            conv_w=conv_weight,
            conv_b=conv_bias,
            w_x=xproj_weight,
            w_dt=dt_weight,
            dt_b=dt_bias,
            a_log=a_log,
            skip=skip_gain,
            w_out=out_weight,
        ),
    )
    if not z.shared:
        r.smalls = lax.psum(r.smalls, "dp")
    g_in, g_out, rest = weight_grads(z, r)
    block_out, input_grad, gains, g_x, g_dt, g_alog, g_conv_w = rest[:7]
    g_conv_b, g_bias, g_skip = rest[7:]
    return (
        block_out,
        input_grad,
        gains,
        g_in,
        g_conv_w,
        g_conv_b,
        g_x,
        g_dt,
        g_bias,
        g_alog,
        g_skip,
        g_out,
    )


def solution(mesh):
    return jax.shard_map(
        functools.partial(local, mesh),
        mesh=mesh,
        in_specs=(
            P("dp", "chan"),
            P(None, "chan"),
            P(None, None, None, "chan"),
            P(None, None, "chan"),
            P(None, "chan"),
            P(None, None, "chan"),
            P(None, None, "chan"),
            P(None, "chan"),
            P(None, None, "chan"),
            P(None, "chan"),
            P(None, "chan", None),
            P(),
            P("dp"),
            P("dp", "chan"),
        ),
        out_specs=(
            P("dp", "chan"),
            P("dp", "chan"),
            P(None, "chan"),
            P(None, None, None, "chan"),
            P(None, None, "chan"),
            P(None, "chan"),
            P(None, None, "chan"),
            P(None, None, "chan"),
            P(None, "chan"),
            P(None, None, "chan"),
            P(None, "chan"),
            P(None, "chan", None),
        ),
        check_vma=False,
    )
```

time: 2230 us -> 202 us (0.09); the launches traced: 2190 us -> 200 us
  local copies, waits for them, and re-layouts: 893 us -> 0 us
  waiting for transfers between devices: 542 us -> 0 us
  other arithmetic: 371 us -> 0 us
  blocking collectives: 328 us -> 0 us
  Pallas kernels: 0 us -> 199 us
  matrix products: 31.1 us -> 0 us
    pad x64 -> x0, local copies, waits for them, and re-layouts: 767 us -> none  [block_scan(): lax.associative_scan(chain_pair, (dec_blocks, drv_blocks), axis=1)]
    psum x2 -> x0, waiting for transfers between devices: 479 us -> none  [local(): lax.psum((g_gain, g_in, g_conv_w, g_conv_b, g_x, g_dt, g_bias, g_alog, g_...]
    all_gather x12 -> x0, blocking collectives: 223 us -> none  [the longest x4 99 us: carried_in(): pieces = jax.tree.map(lambda part: lax.all_gather(part, axis), value)]
    add x80 -> x0, other arithmetic: 206 us -> none  [the longest x40 111 us: block_scan(): lax.associative_scan(chain_pair, (dec_blocks, drv_blocks), axis=1)]
    pallas_call x0 -> x2, Pallas kernels: none -> 199 us  [the longest x1 182 us: run_blocks(): pl.pallas_call(kernel, out_shape=[one[0] for one in trees[1][0]], in_spec...]
    psum x8 -> x0, blocking collectives: 105 us -> none  [the longest x2 58.6 us: layer_backward(): grad_proj = lax.psum(back_part, 'chan').astype(jnp.bfloat16)]
    reduce_scatter x4 -> x0, waiting for transfers between devices: 58.1 us -> none  [the longest x2 42.2 us: layer_forward(): lax.psum_scatter(out_terms, 'chan', scatter_dimension=1, tiled=True)]
    dynamic_update_slice x16 -> x0, other arithmetic: 52.6 us -> none  [block_scan(): last_pair, joined = lax.scan(link, start, (prod_in, acc_in))]
  transfers between devices with their start and end apart: 10 -> 0, of which waited for: 7 -> 0; matrix products, arithmetic and copies ran while one was open for 2% -> 0% of each run, Pallas kernels for 0% -> 0%
where the time goes in v1:
time: 202 us; the launch traced here: 200 us
  Pallas kernels  199 us (99%)
    pallas_call x1, Pallas kernels, run_blocks(): pl.pallas_call(kernel, out_shape=[one[0] for one in trees[1][0]], in_spec...  182 us
    pallas_call x1, Pallas kernels, weight_grads(): pl.pallas_call(kernel, grid=(layers, blocks, steps), out_shape=[shape((la...  16.6 us

profile of v1, /device:TPU:1, one launch (start us, length us, event | category | flops | bytes accessed | tf_op | source)
XLA Modules:
  0.0 199.7 jit_solution(6368942056940484576)
XLA Ops:
  0.6 182.3 %blocks.1 = (f32[128,256]{1,0:T(8,128)}, bf16[2,1024,512]{2,1,0:T(8,128)(2,1)}, bf16[2,1024,512]{2,1,0:T(8,128)(2,1)}, f32[2,256]{1,0:T(2,128)}, bf16[2,512,1024...) custom-call(f32[2,16,512]{2,1,0:T(8,128)} %refs_0_.1, ...), custom_call_target="tpu_custom_call" | custom-call | tf_op jit(solution)/shard_map/blocks/pallas_call | solution.py:1046
  182.9 16.6 %weight_grads.1 = (f32[16384,128]{1,0:T(8,128)}, f32[2,512,1024]{2,1,0:T(8,128)}, f32[128,256]{1,0:T(8,128)}, f32[128,256]{1,0:T(8,128)}, f32[2,256]{1,0:T(2,128...) custom-call(bf16[2,1024,1024]{2,1,0:T(8,128)(2,1)} %get-tuple-elemen, ...), custom_call_target="tpu_custom_call" | custom-call | tf_op jit(solution)/shard_map/weight_grads/pallas_call | solution.py:1126

commit v2 on v1

--- a/solution.py
+++ b/solution.py
@@ -47,8 +47,10 @@
     z.half = z.width // 2
     z.total = z.toks * z.ndp
     z.groups = z.chans // LANES
+    z.chunk = min(256, z.total)
     z.span = 2 * z.groups
-    z.pack = -(-(z.xdim + z.rank + z.states + z.taps + 3) // 128) * 128
+    z.pack = 128
+    assert max(z.xdim + z.taps + 1, z.rank + z.states + 2) <= z.pack
     z.shared = z.pack % (16 * z.ndp) == 0
     z.piece = z.pack // z.ndp if z.shared else z.pack
     return z
@@ -93,13 +95,13 @@
         eland=vm((2 * HALO, c), F32),
         dm=vm((t, 2 * c), BF16),
         ht=vm((z.quarter, t), BF16),
-        gt=vm((c, t), BF16),
+        sct=vm((c, t), BF16),
         gq=vm((t, d), BF16),
         g=vm((t, d), F32),
-        pack=vm((z.pack, c), F32),
-        packb=vm((z.pack, c), BF16),
-        rsland=vm((n, z.piece, c), BF16),
-        small=vm((z.pack, c), BF16),
+        packs=[vm((z.pack, c), F32) for _ in range(2)],
+        packed=[vm((z.pack if z.shared else 16, c), BF16) for _ in range(2)],
+        rsland=[vm((n if z.shared else 1, z.piece, c), BF16) for _ in range(2)],
+        small=[vm((z.pack if z.shared else 16, c), BF16) for _ in range(2)],
         gnsend=vm((8, z.quarter), F32),
         gnland=vm((n, 8, z.quarter), F32),
     )
@@ -129,8 +131,13 @@
         dgated=vm((t, c), F32),
         dc=vm((ext, c), F32),
         grow=vm((8, d), F32),
-        raw=vm((z.layers, d * z.span, LANES), BF16),
+        raw=vm((d * z.span, LANES), BF16),
         stage=vm((LANES * z.span, LANES), F32),
+        hidc=vm((2, d, z.chunk), BF16),
+        gqc=vm((2, z.chunk, d), BF16),
+        scanc=vm((2, c, z.chunk), BF16),
+        gatc=vm((2, c, z.chunk), BF16),
+        dmgc=vm((2, c, z.chunk), BF16),
         wi=vm((z.layers, d, 2 * c), BF16),
         wo=vm((z.layers, c, d), BF16),
     )
@@ -186,42 +193,64 @@
         drains.append(copy.wait_send)
         return copy
 
-    def chan_send(src, dst):
-        return [send(src, dst, (dp, across[p])) for p in (2, 3, 1)]
-
-    def edge_send(pairs, step):
+    def bundle(total, index):
+        return remote(total, total, index, (dp, across[1]))
+
+    def send_all(copies, total):
+        index = alloc(1)
+        for src, dst, target in copies:
+            remote(src, dst, index, target).start()
+        whole = bundle(total, index)
+        drains.append(whole.wait_send)
+        return whole
+
+    def chan_send(src, dst, total):
+        return send_all([(src, dst, (dp, across[p])) for p in (2, 3, 1)], total)
+
+    def edge_send(groups, step):
         there, here = (has_next, has_prev) if step > 0 else (has_prev, has_next)
-        copies = [
-            remote(src, dst, alloc(1), (dp + step, chan)) for src, dst, chan in pairs
-        ]
-
-        @pl.when(there)
-        def _():
-            for copy in copies:
-                copy.start()
+        wholes = []
+        for copies, total in groups:
+            index = alloc(1)
+            wholes.append(bundle(total, index))
+
+            @pl.when(there)
+            def _():
+                for src, dst, chan in copies:
+                    remote(src, dst, index, (dp + step, chan)).start()
 
         def drain():
             @pl.when(there)
             def _():
-                for copy in copies:
-                    copy.wait_send()
+                for whole in wholes:
+                    whole.wait_send()
 
         drains.append(drain)
 
         def arrive():
             @pl.when(here)
             def _():
-                for copy in copies:
-                    copy.wait_recv()
+                for whole in wholes:
+                    whole.wait_recv()
 
         return arrive
 
-    def dp_send(src_of, dst, low, high):
-        base = alloc(n)
-
+    def dp_send_all(src_of, dst, total):
+        index = alloc(1)
+
+        def body(o, carry):
+            to = lax.rem(dp + o, n)
+            remote(src_of(to), dst, index, (to, ch)).start()
+            return carry
+
+        lax.fori_loop(1, n, body, 0)
+        whole = bundle(total, index)
+        drains.append(whole.wait_send)
+        return whole.wait_recv
+
+    def dp_send(src, dst, base, low, high):
         def copy_of(o):
-            to = lax.rem(dp + o, n)
-            return remote(src_of(to), dst, base + o, (to, ch))
+            return remote(src, dst, base + o - 1, (lax.rem(dp + o, n), ch))
 
         def each(act):
             def body(o, carry):
@@ -240,49 +269,37 @@
 
         return arrive
 
-    def gather(src, place):
-        first, second = alloc(nq), alloc(nq)
+    def gather(src, place, total):
+        first, second = alloc(1), alloc(1)
         local = pltpu.make_async_copy(src, place(dp), v.ls.at[alloc_local()])
         local.start()
 
-        def hop(o):
+        def start(o, carry):
             to = lax.rem(rank_q + o, nq) * 2 + pair
-            return remote(src, place(dp), first + o, (to, ch))
-
-        def relay(o):
-            origin = lax.rem(rank_q - o + nq, nq) * 2 + pair
-            return remote(place(origin), place(origin), second + o, (twin, ch))
-
-        own = remote(src, place(dp), second, (twin, ch))
-
-        def start(o, carry):
-            hop(o).start()
+            remote(src, place(dp), first, (to, ch)).start()
             return carry
 
         lax.fori_loop(1, nq, start, 0)
-        own.start()
+        remote(src, place(dp), second, (twin, ch)).start()
 
         def forward():
+            bundle(total(nq - 1), first).wait_recv()
+
             def body(o, carry):
-                hop(o).wait_recv()
-                relay(o).start()
+                origin = lax.rem(rank_q - o + nq, nq) * 2 + pair
+                remote(place(origin), place(origin), second, (twin, ch)).start()
                 return carry
 
             lax.fori_loop(1, nq, body, 0)
 
         def finish():
-            def body(o, carry):
-                hop(o).wait_send()
-                relay(o).wait()
-                return carry
-
-            lax.fori_loop(1, nq, body, 0)
-            own.wait()
+            bundle(total(nq - 1), first).wait_send()
+            bundle(total(nq), second).wait()
             local.wait()
 
         return SimpleNamespace(forward=forward, finish=finish)
 
-    locals_used = [2 * z.layers]
+    locals_used = [2 * z.layers + 10]
 
     def alloc_local():
         locals_used[0] += 1
@@ -294,14 +311,14 @@
             (
                 pltpu.make_async_copy(
                     v.w_in.at[pl.ds(l * d * z.span, d * z.span), :],
-                    v.raw.at[l],
+                    v.raw,
                     v.ls.at[2 * l],
                 ),
                 pltpu.make_async_copy(v.w_out.at[l], v.wo.at[l], v.ls.at[2 * l + 1]),
             )
         )
-        for copy in loads[l]:
-            copy.start()
+        loads[l][1].start()
+    loads[0][0].start()
 
     def load_in(l):
         loads[l][0].wait()
@@ -310,7 +327,7 @@
         def body(k, carry):
             at = pl.ds(pl.multiple_of(k * rows, rows), rows)
             to = pl.ds(pl.multiple_of(k * LANES, LANES), LANES)
-            v.stage[...] = v.raw[l, at, :].astype(F32)
+            v.stage[...] = v.raw[at, :].astype(F32)
             for g in range(groups):
                 for side_of in range(2):
                     col = side_of * c + g * LANES
@@ -320,6 +337,8 @@
             return carry
 
         lax.fori_loop(0, d // LANES, body, 0)
+        if l + 1 < z.layers:
+            loads[l + 1][0].start()
 
     barrier = pltpu.get_barrier_semaphore()
     for p in (1, 2, 3):
@@ -374,19 +393,20 @@
     head = pl.ds(0, HALO)
     tail = pl.ds(t - HALO, HALO)
     everyone = [ch, across[1], across[2], across[3]]
-    got_h = chan_send(v.hq, L[0].hid.at[own, q_cols])
-    got_m = chan_send(v.meta, v.metas.at[ch])
+    got_h = chan_send(
+        v.hq, L[0].hid.at[own, q_cols], L[0].hid.at[own, 0 : 3 * quarter]
+    )
+    got_m = chan_send(v.meta, v.metas.at[ch], v.metas.at[0 : z.nch - 1])
     got_edge = edge_send(
-        [(v.hq.at[tail, :], L[0].hid.at[head, q_cols], k) for k in everyone]
-        + [(v.meta, v.metah.at[ch], k) for k in everyone],
+        [
+            (
+                [(v.hq.at[tail, :], L[0].hid.at[head, q_cols], k) for k in everyone],
+                L[0].hid.at[head, :],
+            ),
+            ([(v.meta, v.metah.at[ch], k) for k in everyone], v.metah),
+        ],
         1,
     )
-    got_x = chan_send(v.x, L[0].xs.at[own, q_cols])
-    got_xedge = edge_send(
-        [(v.x.at[tail, :], L[0].xs.at[head, q_cols], k) for k in everyone], 1
-    )
-    got_c = chan_send(v.cq, L[1].gq.at[:, q_cols])
-    got_g = chan_send(v.cot, L[1].g.at[:, q_cols])
     L[0].hid[own, q_cols] = v.hq[...]
     v.metas[ch] = v.meta[...]
     L[0].xs[own, q_cols] = xq
@@ -414,9 +434,10 @@
 
     def fwd_head(l):
         hid, inv = L[l].hid, L[l].inv
-        scale = wide(inv[...], c)
-        mixed = dot(hid[...], v.wi[l, :, 0:c])
-        inner = (scale * mixed).astype(BF16).astype(F32)
+        inner = dot(hid[...], v.wi[l, :, 0:c])
+        if l == 0:
+            inner = wide(inv[...], c) * inner
+        inner = inner.astype(BF16).astype(F32)
         L[l].inner[...] = inner
         conv = jnp.broadcast_to(v.conv_b[l : l + 1, :], (t, c))
         for k in range(z.taps):
@@ -429,16 +450,19 @@
         L[l].actf[...] = act.astype(F32)
         part = dot(v.w_x[l], act, ((1,), (1,))).astype(BF16)
         L[l].psend[...] = part
-        got = chan_send(L[l].psend, L[l].pland.at[ch])
+        land = L[l].pland
+        got = chan_send(L[l].psend, land.at[ch], land.at[0 : z.nch - 1])
         L[l].pland[ch] = part
         L[l].slope[...] = silu_slope(conv, sig)
         gate = dot(hid[own, :], v.wi[l, :, c : 2 * c])
-        L[l].gate[...] = (wide(inv[own, :], c) * gate).astype(BF16).astype(F32)
+        if l == 0:
+            gate = wide(inv[own, :], c) * gate
+        gate = gate.astype(BF16)
+        L[l].gate[...] = gate.astype(F32)
         return got
 
     def fwd_mid(l, got):
-        for copy in got:
-            copy.wait_recv()
+        got.wait_recv()
         land = L[l].pland
         proj = land[0].astype(F32)
         for k in range(1, z.nch):
@@ -455,7 +479,8 @@
         L[l].ssend[...] = jnp.broadcast_to(
             jnp.sum(stepk, axis=0, keepdims=True), (8, c)
         )
-        got_s = dp_send(lambda to: L[l].ssend, L[l].ssum.at[dp], 1, n)
+        land = L[l].ssum
+        got_s = dp_send_all(lambda to: L[l].ssend, land.at[dp], land.at[0 : n - 1])
         bc = proj[rank : rank + 2 * ns, :]
         lanes = lax.broadcasted_iota(jnp.int32, (2 * ns, t), 1)
         bce = L[l].bce
@@ -554,6 +579,7 @@
         )
         scanned = y[...] + v.skip[l : l + 1, :] * L[l].actf[...]
         y[...] = scanned
+        L[l].sct[...] = jnp.transpose(scanned.astype(BF16))
         gate = L[l].gate[...]
         gated = (scanned * gate * jax.nn.sigmoid(gate)).astype(BF16)
         L[l].gated[...] = gated
@@ -578,8 +604,13 @@
         if edge:
             arrive = edge_send(
                 [
-                    (b_send.at[tail, :], v.b_halo.at[side], chan)
-                    for chan in (ch, across[2])
+                    (
+                        [
+                            (b_send.at[tail, :], v.b_halo.at[side], chan)
+                            for chan in (ch, across[2])
+                        ],
+                        v.b_halo,
+                    )
                 ],
                 1,
             )
@@ -617,9 +648,7 @@
         gate = L[l].gate[...]
         sig = jax.nn.sigmoid(gate)
         dgate = v.dgated[...] * L[l].scan[...] * silu_slope(gate, sig)
-        L[l].dm[:, c : 2 * c] = (wide(L[l].inv[own, :], c) * dgate).astype(
-            BF16
-        )
+        L[l].dm[:, c : 2 * c] = dgate.astype(BF16)
 
     def back_scan(l, flow_in):
         a = a_of(l)
@@ -678,13 +707,12 @@
                 jnp.zeros((ns, t), F32),
             ),
         )
-        at = z.xdim + rank
         for g in range(groups):
-            L[l].pack[at : at + ns, lane(g)] = acc[g] * a[:, lane(g)]
+            L[l].packs[0][rank : rank + ns, lane(g)] = acc[g] * a[:, lane(g)]
         return acc_b, acc_c
 
     def back_mid(l, acc_b, acc_c):
-        pack = L[l].pack
+        pack = L[l].packs[0]
         actf = L[l].actf[...]
         ds = L[l].ds[...]
         dpre = v.dst[...] * jax.nn.sigmoid(L[l].pre[...])
@@ -693,23 +721,25 @@
         bsend[0:rank, :] = dot(v.w_dt[l], dpre_q, ((1,), (1,))).astype(BF16)
         bsend[rank : rank + ns, :] = acc_b.astype(BF16)
         bsend[rank + ns : rank + 2 * ns, :] = acc_c.astype(BF16)
-        got = chan_send(bsend, L[l].bland.at[ch])
-        L[l].bland[ch] = bsend[...]
+        land = L[l].bland
+        got = chan_send(bsend, land.at[ch], land.at[0 : z.nch - 1])
+        land[ch] = bsend[...]
         dact = ds * v.skip[l : l + 1, :] + L[l].step[...] * v.adj[...]
         v.dact[...] = dact
         L[l].esend[0:HALO, :] = dact[0:HALO, :]
         L[l].esend[HALO : 2 * HALO, :] = L[l].slope[0:HALO, :]
         edge = edge_send(
-            [(L[l].esend, L[l].eland, ch)]
-            + [(bsend, L[l].bhalo.at[ch], k) for k in everyone],
+            [
+                ([(L[l].esend, L[l].eland, ch)], L[l].eland),
+                ([(bsend, L[l].bhalo.at[ch], k) for k in everyone], L[l].bhalo),
+            ],
             -1,
         )
-        pack[z.xdim : z.xdim + rank, :] = dot(L[l].stept[...], dpre_q)
-        at = z.xdim + rank + ns + z.taps
-        pack[at + 1 : at + 2, :] = jnp.sum(dpre, axis=0, keepdims=True)
-        pack[at + 2 : at + 3, :] = jnp.sum(ds * actf, axis=0, keepdims=True)
-        if at + 3 < z.pack:
-            pack[at + 3 :, :] = jnp.zeros((z.pack - at - 3, c), F32)
+        pack[0:rank, :] = dot(L[l].stept[...], dpre_q)
+        at = rank + ns
+        pack[at : at + 1, :] = jnp.sum(dpre, axis=0, keepdims=True)
+        pack[at + 1 : at + 2, :] = jnp.sum(ds * actf, axis=0, keepdims=True)
+        pack[at + 2 :, :] = jnp.zeros((z.pack - at - 2, c), F32)
         return got, edge
 
     def sum_land(ref):
@@ -719,9 +749,7 @@
         return total.astype(BF16)
 
     def back_conv(l, got, edge):
-        pack = L[l].pack
-        for copy in got:
-            copy.wait_recv()
+        got.wait_recv()
         edge()
         dproj = sum_land(L[l].bland)
         dproj_h = sum_land(L[l].bhalo)
@@ -740,78 +768,80 @@
             dinner = dinner + (
                 term if k == z.taps - 1 else term * valid(k, rows, c)
             )
-        L[l].dm[:, 0:c] = (wide(L[l].inv[own, :], c) * dinner).astype(BF16)
+        L[l].dm[:, 0:c] = dinner.astype(BF16)
         return dproj
 
     def back_rest(l, dproj):
-        pack = L[l].pack
+        pack = L[l].packs[1]
         pack[0 : z.xdim, :] = dot(dproj, L[l].act[...])
         dconv = v.dc[0:t, :]
-        at = z.xdim + rank + ns
+        at = z.xdim
         for k in range(z.taps):
             row = HALO - z.taps + 1 + k
             term = dconv * L[l].inner[row : row + t, :]
             if k < z.taps - 1:
                 term = term * valid(k, slice(0, t), c)
             pack[at + k : at + k + 1, :] = jnp.sum(term, axis=0, keepdims=True)
-        pack[at + z.taps : at + z.taps + 1, :] = jnp.sum(dconv, axis=0, keepdims=True)
+        at = at + z.taps
+        pack[at : at + 1, :] = jnp.sum(dconv, axis=0, keepdims=True)
+        pack[at + 1 :, :] = jnp.zeros((z.pack - at - 1, c), F32)
 
     def back_norm(l, k):
-        u = R[k].full[own, :]
+        inv = wide(L[l].inv[own, :], d)
+        u = R[k].full[own, :] * inv
         x = L[l].xs[own, :]
         scaled = u * v.gfull[l : l + 1, :]
-        xhat = x * wide(L[l].inv[own, :], d)
+        xhat = x * inv
         mean = jnp.sum(scaled * xhat, axis=1, keepdims=True) * (1.0 / d)
         v.grow[...] = jnp.broadcast_to(jnp.sum(u * x, axis=0, keepdims=True), (8, d))
         L[l].gnsend[...] = v.grow[:, q_cols]
         L[l].gnland[dp] = v.grow[:, q_cols]
-        arrive = dp_send(
-            lambda to: L[l].gnsend, L[l].gnland.at[dp], 1, n
-        )
+        land = L[l].gnland
+        arrive = dp_send_all(lambda to: L[l].gnsend, land.at[dp], land.at[0 : n - 1])
         return L[l].g[...] + scaled - xhat * mean, arrive
 
     def gain_out(l, arrive):
-        arrive(1, n)
+        arrive()
         total = lax.fori_loop(
             0, n, lambda j, s: s + L[l].gnland[j], jnp.zeros((8, quarter), F32)
         )
         v.gains[l : l + 1, :] = total[0:1, :]
 
-    def small_scatter(l):
+    def small_scatter(l, p):
         if not z.shared:
-            v.smalls[l] = L[l].pack[...]
+            v.smalls[l, p] = L[l].packs[p][...]
             return None
         rows = z.piece
-        packb = L[l].packb
-        packb[...] = L[l].pack[...].astype(BF16)
+        packed, land = L[l].packed[p], L[l].rsland[p]
+        packed[...] = L[l].packs[p][...].astype(BF16)
         piece = lambda j: pl.ds(pl.multiple_of(j * rows, rows), rows)
-        arrive = dp_send(
-            lambda to: packb.at[piece(to), :], L[l].rsland.at[dp], 1, n
-        )
-        L[l].rsland[dp] = packb[piece(dp), :]
+        arrive = dp_send_all(
+            lambda to: packed.at[piece(to), :], land.at[dp], land.at[0 : n - 1]
+        )
+        land[dp] = packed[piece(dp), :]
         return arrive
 
-    def small_gather(l, arrive):
+    def small_gather(l, p, arrive):
         if not z.shared:
             return None
         rows = z.piece
-        arrive(1, n)
+        small, land = L[l].small[p], L[l].rsland[p]
+        arrive()
         total = lax.fori_loop(
-            0,
-            n,
-            lambda j, s: s + L[l].rsland[j].astype(F32),
-            jnp.zeros((rows, c), F32),
+            0, n, lambda j, s: s + land[j].astype(F32), jnp.zeros((rows, c), F32)
         )
         mine = pl.ds(pl.multiple_of(dp * rows, rows), rows)
-        L[l].small[mine, :] = total.astype(BF16)
-        return dp_send(
-            lambda to: L[l].small.at[mine, :], L[l].small.at[mine, :], 1, n
-        )
-
-    def small_out(l, arrive):
+        small[mine, :] = total.astype(BF16)
+        return dp_send_all(
+            lambda to: small.at[mine, :],
+            small.at[mine, :],
+            small.at[0 : (n - 1) * rows, :],
+        )
+
+    def small_out(l, p, arrive):
         if z.shared:
-            arrive(1, n)
-            v.smalls[l] = L[l].small[...]
+            arrive()
+            v.smalls[l, p] = L[l].small[p][...]
 
     def inverse(total):
         return lax.rsqrt(total * (1.0 / d) + EPSILON)
@@ -830,183 +860,288 @@
             jnp.transpose(inverse(sums_h))[t - HALO : t, 0:1], (HALO, LANES)
         )
 
-    def lanes_at(l, ref, rows):
-        return lambda j: ref.at[l, rows, pl.ds(pl.multiple_of(j * t, t), t)]
-
-    def rows_at(l, ref, cols, low=0, high=t):
-        return lambda j: ref.at[
-            l, pl.ds(pl.multiple_of(j * t + low, high - low), high - low), cols
-        ]
+    def in_lanes(src, ref, l, rows):
+        return gather(
+            src,
+            lambda j: ref.at[l, rows, pl.ds(pl.multiple_of(j * t, t), t)],
+            lambda count: ref.at[l, rows, 0 : count * t],
+        )
+
+    def in_rows(src, ref, l, cols, low=0, high=t):
+        m = high - low
+        return gather(
+            src,
+            lambda j: ref.at[l, pl.ds(pl.multiple_of(j * t + low, m), m), cols],
+            lambda count: ref.at[l, 0 : count * m, cols],
+        )
 
     def gather_hid(l):
-        L[l].ht[...] = jnp.transpose(L[l].hid[own, q_cols])
-        return gather(L[l].ht, lanes_at(l, v.hid_all, q_cols))
-
-    def gather_gat(l):
-        L[l].gt[...] = jnp.transpose(L[l].gated[...])
-        return gather(L[l].gt, lanes_at(l, v.gat_all, slice(None)))
+        if l == 0:
+            hidden = xq * v.gain[0:1, :] * wide(L[0].inv[own, :], quarter)
+            L[0].ht[...] = jnp.transpose(hidden.astype(BF16))
+        else:
+            L[l].ht[...] = jnp.transpose(L[l].hid[own, q_cols])
+        return in_lanes(L[l].ht, v.hid_all, l, q_cols)
+
+    def gather_scan(l):
+        return in_lanes(L[l].sct, v.scan_all, l, slice(None))
 
     def gather_gq(l):
-        return gather(L[l].gq.at[:, q_cols], rows_at(l, v.gq_all, q_cols))
-
-    def gather_dmg(l):
-        cols = slice(c, 2 * c)
-        return gather(L[l].dm.at[:, cols], rows_at(l, v.dmg_all, slice(None)))
+        return in_rows(L[l].gq.at[:, q_cols], v.gq_all, l, q_cols)
 
     def gather_dmi(l, low=0, high=t):
         src = L[l].dm.at[low:high, 0:c]
-        return gather(src, rows_at(l, v.dmi_all, slice(None), low, high))
+        return in_rows(src, v.dmi_all, l, slice(None), low, high)
 
     def quarter_at(k):
         return pl.ds(pl.multiple_of(k * quarter, quarter), quarter)
 
-    def share(region):
+    def share(region, total):
         mine = region(ch)
         got = send(mine, mine, (dp, across[2]))
 
         def second():
             got.wait_recv()
             theirs = region(across[2])
-            one = send(mine, mine, (dp, across[1]))
-            two = send(theirs, theirs, (dp, across[1]))
-
-            def done():
-                one.wait_recv()
-                two.wait_recv()
-
-            return done
+            to = (dp, across[1])
+            return send_all([(mine, mine, to), (theirs, theirs, to)], total).wait_recv
 
         return second
 
     def share_hid(l):
-        return share(lambda k: v.hid_all.at[l, quarter_at(k), :])
+        return share(
+            lambda k: v.hid_all.at[l, quarter_at(k), :],
+            v.hid_all.at[l, 0 : 2 * quarter, :],
+        )
 
     def share_gq(l):
-        return share(lambda k: v.gq_all.at[l, :, quarter_at(k)])
-
-    hid0 = gather_hid(0)
-    gq1 = gather_gq(1)
+        return share(
+            lambda k: v.gq_all.at[l, :, quarter_at(k)],
+            v.gq_all.at[l, :, 0 : 2 * quarter],
+        )
+
+    def share_rows(ref, rows):
+        return share(lambda k: ref.at[rows, quarter_at(k)], ref.at[rows, 0 : 2 * quarter])
+
+    chunks = z.total // z.chunk
+
+    def chunk_loads(l, k):
+        slot = lax.rem(k, 2)
+        base = 2 * z.layers + 5 * slot
+        at = pl.ds(pl.multiple_of(k * z.chunk, z.chunk), z.chunk)
+        pairs = (
+            (v.hid_all.at[l, :, at], v.hidc.at[slot]),
+            (v.gq_all.at[l, at, :], v.gqc.at[slot]),
+            (v.scan_all.at[l, :, at], v.scanc.at[slot]),
+        )
+        return [
+            pltpu.make_async_copy(src, to, v.ls.at[base + i])
+            for i, (src, to) in enumerate(pairs)
+        ]
+
+    def chunk_stores(l, k):
+        slot = lax.rem(k, 2)
+        base = 2 * z.layers + 5 * slot + 3
+        at = pl.ds(pl.multiple_of(k * z.chunk, z.chunk), z.chunk)
+        pairs = (
+            (v.gatc.at[slot], v.gat_all.at[l, :, at]),
+            (v.dmgc.at[slot], v.dmg_all.at[l, :, at]),
+        )
+        return [
+            pltpu.make_async_copy(src, to, v.ls.at[base + i])
+            for i, (src, to) in enumerate(pairs)
+        ]
+
+    def finish_begin(l):
+        for copy in chunk_loads(l, jnp.int32(0)):
+            copy.start()
+
+    def finish_some(l, low, high):
+        def body(k, carry):
+            slot = lax.rem(k, 2)
+
+            @pl.when(k + 1 < chunks)
+            def _():
+                for copy in chunk_loads(l, k + 1):
+                    copy.start()
+
+            @pl.when(k >= 2)
+            def _():
+                for copy in chunk_stores(l, k - 2):
+                    copy.wait()
+
+            loads_in = chunk_loads(l, k)
+            loads_in[0].wait()
+            w_gate = v.wi[l, :, c : 2 * c]
+            gate = dot(w_gate, v.hidc[slot], ((0,), (0,))).astype(BF16).astype(F32)
+            loads_in[1].wait()
+            dgated = dot(v.wo[l], v.gqc[slot], ((1,), (1,)))
+            loads_in[2].wait()
+            scanned = v.scanc[slot].astype(F32)
+            sig = jax.nn.sigmoid(gate)
+            v.gatc[slot] = (scanned * gate * sig).astype(BF16)
+            v.dmgc[slot] = (dgated * scanned * silu_slope(gate, sig)).astype(BF16)
+            for copy in chunk_stores(l, k):
+                copy.start()
+            return carry
+
+        lax.fori_loop(low, high, body, 0)
+
+    def finish_end(l):
+        for k in range(max(chunks - 2, 0), chunks):
+            for copy in chunk_stores(l, jnp.int32(k)):
+                copy.wait()
+
     load_in(0)
-    for copy in got_h + got_m:
-        copy.wait_recv()
+    got_h.wait_recv()
+    got_m.wait_recv()
     got_edge()
     norms()
     got_p = fwd_head(0)
+    share_x = share_rows(L[0].xs, own)
+    share_c = share_rows(L[1].gq, slice(None))
+    got_xedge = edge_send(
+        [
+            (
+                [(v.x.at[tail, :], L[0].xs.at[head, q_cols], k) for k in everyone],
+                L[0].xs.at[head, :],
+            )
+        ],
+        1,
+    )
+    hid0 = gather_hid(0)
+    gq1 = gather_gq(1)
     load_in(1)
     got_s0 = fwd_mid(0, got_p)
     put(L[0].carry, 0, scan_sum(0))
-    got_carry = dp_send(lambda to: L[0].carry.at[0], L[0].sland.at[dp], 1, n - dp)
-    for copy in got_x + got_c + got_g:
-        copy.wait_recv()
-    got_xedge()
+    got_carry = dp_send(L[0].carry.at[0], L[0].sland.at[dp], alloc(n - 1), 1, n - dp)
+    share_x = share_x()
+    share_c = share_c()
+    share_g = share_rows(L[1].g, slice(None))
     loads[0][1].wait()
-    got_s0(1, n)
+    got_s0()
     got_carry(1, dp + 1)
     hid0.forward()
     gq1.forward()
     scan_out(0, carry_in(0, L[0].sland, lambda k: k, dp))
+    scan0 = gather_scan(0)
     red0 = reduce_a(0, out_part(0))
-    gat0 = gather_gat(0)
     red0, arrive = reduce_b(0, red0, True)
-    reduce_c(0, red0, arrive).wait_recv()
+    share_g = share_g()
+    got_c = reduce_c(0, red0, arrive)
+    share_x()
+    got_xedge()
+    got_c.wait_recv()
     x1 = L[0].xs[...] + R[0].full[...]
     L[1].xs[...] = x1
-    L[1].hid[...] = (x1 * v.gfull[1:2, :]).astype(BF16)
-    L[1].inv[...] = jnp.broadcast_to(
-        inverse(jnp.sum(x1 * x1, axis=1, keepdims=True)), (ext, LANES)
-    )
+    inv1 = inverse(jnp.sum(x1 * x1, axis=1, keepdims=True))
+    L[1].hid[...] = (x1 * inv1 * v.gfull[1:2, :]).astype(BF16)
+    L[1].inv[...] = jnp.broadcast_to(inv1, (ext, LANES))
 
     got_p = fwd_head(1)
     hid1 = gather_hid(1)
-    gat0.forward()
+    scan0.forward()
     loads[1][1].wait()
+    share_c()
     back_gate(1)
     got_s1 = fwd_mid(1, got_p)
     hid0.finish()
     share0 = share_hid(0)
     put(L[1].carry, 0, scan_sum(1))
     put(L[1].carry, 1, back_sum(1))
-    got_f = dp_send(lambda to: L[1].carry.at[0], L[1].sland.at[dp], 1, n - dp)
-    got_r = dp_send(lambda to: L[1].carry.at[1], L[1].rland.at[dp], n - dp, n)
-    got_s1(1, n)
+    base = alloc(n - 1)
+    got_f = dp_send(L[1].carry.at[0], L[1].sland.at[dp], base, 1, n - dp)
+    got_r = dp_send(L[1].carry.at[1], L[1].rland.at[dp], base, n - dp, n)
+    got_s1()
     got_f(1, dp + 1)
     got_r(dp + 1, n)
     hid1.forward()
     gq1.finish()
     share1 = share_gq(1)
     scan_out(1, carry_in(1, L[1].sland, lambda k: k, dp))
-    gat1 = gather_gat(1)
+    scan1 = gather_scan(1)
     back_dgate(1)
-    dmg1 = gather_dmg(1)
     red1 = reduce_a(1, out_part(1))
 
     acc_b, acc_c = back_scan(1, carry_in(1, L[1].rland, lambda k: n - 1 - k, n - 1 - dp))
     got_b, edge = back_mid(1, acc_b, acc_c)
     share0 = share0()
     red1, _ = reduce_b(1, red1, False)
-    gat1.forward()
     dproj = back_conv(1, got_b, edge)
     red2 = reduce_a(2, in_part(1))
-    dmg1.forward()
     dmi1 = gather_dmi(1)
     back_rest(1, dproj)
     red2, _ = reduce_b(2, red2, False)
     share1 = share1()
     reduce_c(1, red1, None).wait_recv()
+    share1()
     v.block_out[...] = L[1].xs[own, q_cols] + R[1].full[own, q_cols]
+    scan1.forward()
     reduce_c(2, red2, None).wait_recv()
+    share_g()
     grad, gain1 = back_norm(1, 2)
     L[0].g[...] = grad
     L[0].gq[...] = grad.astype(BF16)
 
     back_gate(0)
     put(L[0].carry, 1, back_sum(0))
-    got_r = dp_send(lambda to: L[0].carry.at[1], L[0].rland.at[dp], n - dp, n)
-    gq0 = gather_gq(0)
+    got_r = dp_send(L[0].carry.at[1], L[0].rland.at[dp], alloc(n - 1), n - dp, n)
     back_dgate(0)
     hid1.finish()
     share2 = share_hid(1)
     got_r(dp + 1, n)
-    dmg0 = gather_dmg(0)
+    gq0 = gather_gq(0)
     dmi1.forward()
-    small1 = small_scatter(1)
+    small1 = [small_scatter(1, 0), small_scatter(1, 1)]
     acc_b, acc_c = back_scan(0, carry_in(0, L[0].rland, lambda k: n - 1 - k, n - 1 - dp))
     got_b, edge = back_mid(0, acc_b, acc_c)
     share2 = share2()
+    small0 = [small_scatter(0, 0)]
     gq0.forward()
     dproj = back_conv(0, got_b, edge)
     dmi0 = [gather_dmi(0, 0, t // 2), gather_dmi(0, t // 2, t)]
     red3 = reduce_a(3, in_part(0))
-    dmg0.forward()
     back_rest(0, dproj)
-    small0 = small_scatter(0)
-    small1 = small_gather(1, small1)
+    small0.append(small_scatter(0, 1))
     red3, _ = reduce_b(3, red3, False)
+    small1 = [small_gather(1, p, small1[p]) for p in range(2)]
+    share2()
+    scan1.finish()
+    finish_begin(1)
     gq0.finish()
-    dmi0[0].forward()
-    reduce_c(3, red3, None).wait_recv()
     share3 = share_gq(0)
+    finish_some(1, 0, chunks // 2)
+    got_c = reduce_c(3, red3, None)
+    finish_some(1, chunks // 2, chunks)
+    got_c.wait_recv()
     grad, gain0 = back_norm(0, 3)
     L[0].g[...] = grad
     v.input_grad[...] = L[0].g[:, q_cols]
+    dmi0[0].forward()
+    share3 = share3()
+    share0()
+    scan0.finish()
+    share3()
+    finish_end(1)
+    finish_begin(0)
+    small0 = [small_gather(0, p, small0[p]) for p in range(2)]
     dmi0[1].forward()
-    small0 = small_gather(0, small0)
-    share3 = share3()
+    finish_some(0, 0, chunks)
+    finish_end(0)
     gain_out(0, gain0)
     gain_out(1, gain1)
-    small_out(1, small1)
-    small_out(0, small0)
-    for one in (share0, share1, share2, share3):
-        one()
-    for one in (gat0, gat1, dmg1, dmi1, dmg0, *dmi0):
+    for p in range(2):
+        small_out(1, p, small1[p])
+        small_out(0, p, small0[p])
+    for one in (dmi1, *dmi0):
         one.finish()
     for drain in drains:
         drain()
-    assert counter[0] <= sems[0] and locals_used[0] <= sems[1], (counter, locals_used)
+    assert (counter[0], locals_used[0]) == sems, (counter, locals_used)
 
 
 def run_blocks(z, args):
-    sems = (160 + 11 * 2 * (z.ndp // 2) + 13 * z.ndp, 4 + 11)
+    sems = (62 + 3 * (z.ndp - 1) + (8 if z.shared else 0), 23)
     vmem = pl.BlockSpec(memory_space=pltpu.VMEM)
     smem = pl.BlockSpec(memory_space=pltpu.SMEM)
     anywhere = pl.BlockSpec(memory_space=pl.ANY)
@@ -1018,13 +1153,14 @@
     outs = dict(
         block_out=(shape((t, z.quarter), F32), vmem),
         input_grad=(shape((t, z.quarter), F32), vmem),
-        smalls=(shape((layers, z.pack, c), BF16 if z.shared else F32), vmem),
+        smalls=(shape((layers, 2, z.pack, c), BF16 if z.shared else F32), vmem),
         gains=(shape((layers, z.quarter), F32), vmem),
         hid_all=(shape((layers, d, n), BF16), anywhere),
         gat_all=(shape((layers, c, n), BF16), anywhere),
+        dmg_all=(shape((layers, c, n), BF16), anywhere),
+        scan_all=(shape((layers, c, n), BF16), anywhere),
         gq_all=(shape((layers, n, d), BF16), anywhere),
         dmi_all=(shape((layers, n, c), BF16), anywhere),
-        dmg_all=(shape((layers, n, c), BF16), anywhere),
     )
     scratch = scratch_of(z)
     flags = dict(
@@ -1057,14 +1193,14 @@
     return SimpleNamespace(**jax.tree.unflatten(trees[1][1], results))
 
 
-def grad_kernel(z, steps, hid, gat, gq, dmi, dmg, smalls, small_ins, win, wout, *outs):
+def grad_kernel(z, steps, ins, small_ins, win, wout, outs):
+    hid, gat, dmg, gq, dmi, smalls = ins
     rows = hid.shape[1]
     first = pl.program_id(2) == 0
     lhs = hid[0]
-    groups = z.groups
-    for k, rhs in enumerate((dmi, dmg)):
-        part = dot(lhs, rhs[0])
-        for j in range(groups):
+    parts = (dot(lhs, dmi[0]), dot(lhs, dmg[0], ((1,), (1,))))
+    for k, part in enumerate(parts):
+        for j in range(z.groups):
             at = pl.ds(j * 2 + k, rows, stride=z.span)
             piece = part[:, j * LANES : (j + 1) * LANES]
             if steps == 1:
@@ -1083,20 +1219,22 @@
     def _():
         for src, to in zip(small_ins, outs[:3], strict=True):
             to[...] = src[...]
-        at = 0
-        for to in outs[3:]:
+        at, pack = 0, 0
+        for i, to in enumerate(outs[3:]):
+            if i == 4:
+                at, pack = 0, 1
             for l in range(z.layers):
                 if len(to.shape) == 3:
                     count = to.shape[1]
-                    to[l] = smalls[l, at : at + count, :].astype(F32)
+                    to[l] = smalls[l, pack, at : at + count, :].astype(F32)
                 else:
                     count = 1
-                    to[l : l + 1, :] = smalls[l, at : at + 1, :].astype(F32)
+                    to[l : l + 1, :] = smalls[l, pack, at : at + 1, :].astype(F32)
             at += count
 
 
 def weight_grads(z, r):
-    blocks = 4
+    blocks = 2
     deep = min(z.total, 1024)
     steps = z.total // deep
     layers, d, c = z.layers, z.width, z.chans
@@ -1106,12 +1244,12 @@
         r.block_out,
         r.input_grad,
         r.gains,
-        shape((layers, z.xdim, c), F32),
         shape((layers, z.rank, c), F32),
         shape((layers, z.states, c), F32),
-        shape((layers, z.taps, c), F32),
         shape((layers, c), F32),
         shape((layers, c), F32),
+        shape((layers, z.xdim, c), F32),
+        shape((layers, z.taps, c), F32),
         shape((layers, c), F32),
     )
 
@@ -1119,9 +1257,9 @@
         dims = len(one.shape)
         return pl.BlockSpec(one.shape, lambda l, i, k: (0,) * dims)
 
-    def kernel(hid, gat, gq, dmi, dmg, smalls, block_out, input_grad, gains, *outs):
-        ins = (block_out, input_grad, gains)
-        grad_kernel(z, steps, hid, gat, gq, dmi, dmg, smalls, ins, *outs)
+    def kernel(*refs):
+        ins, small_ins, (win, wout), outs = refs[:6], refs[6:9], refs[9:11], refs[11:]
+        grad_kernel(z, steps, ins, small_ins, win, wout, outs)
 
     win, wout, *rest = pl.pallas_call(
         kernel,
@@ -1134,8 +1272,8 @@
         in_specs=[
             pl.BlockSpec((1, rows, deep), lambda l, i, k: (l, i, k)),
             pl.BlockSpec((1, orow, deep), lambda l, i, k: (l, i, k)),
+            pl.BlockSpec((1, c, deep), lambda l, i, k: (l, 0, k)),
             pl.BlockSpec((1, deep, d), lambda l, i, k: (l, k, 0)),
-            pl.BlockSpec((1, deep, c), lambda l, i, k: (l, k, 0)),
             pl.BlockSpec((1, deep, c), lambda l, i, k: (l, k, 0)),
             fixed(r.smalls),
             fixed(r.block_out),
@@ -1147,14 +1285,14 @@
             pl.BlockSpec((1, orow, d), lambda l, i, k: (l, i, 0)),
             *[fixed(one) for one in small_shapes],
         ],
-        compiler_params=pltpu.CompilerParams(vmem_limit_bytes=56 * 2**20),
+        compiler_params=pltpu.CompilerParams(vmem_limit_bytes=60 * 2**20),
         name="weight_grads",
     )(
         r.hid_all,
         r.gat_all,
+        r.dmg_all,
         r.gq_all,
         r.dmi_all,
-        r.dmg_all,
         r.smalls,
         r.block_out,
         r.input_grad,
@@ -1206,8 +1344,8 @@
     if not z.shared:
         r.smalls = lax.psum(r.smalls, "dp")
     g_in, g_out, rest = weight_grads(z, r)
-    block_out, input_grad, gains, g_x, g_dt, g_alog, g_conv_w = rest[:7]
-    g_conv_b, g_bias, g_skip = rest[7:]
+    block_out, input_grad, gains, g_dt, g_alog, g_bias, g_skip = rest[:7]
+    g_x, g_conv_w, g_conv_b = rest[7:]
     return (
         block_out,
         input_grad,

time: 202 us -> 174 us (0.86); the launches traced: 200 us -> 174 us
  Pallas kernels: 199 us -> 173 us
    pallas_call x1, Pallas kernels: 182 us -> 157 us  [run_blocks(): pl.pallas_call(kernel, out_shape=[one[0] for one in trees[1][0]], in_spec...]
where the time goes in v2:
time: 174 us
  Pallas kernels  173 us (99%)
    pallas_call x1, Pallas kernels, run_blocks(): pl.pallas_call(kernel, out_shape=[one[0] for one in trees[1][0]], in_spec...  157 us
    pallas_call x1, Pallas kernels, weight_grads(): pl.pallas_call(kernel, grid=(layers, blocks, steps), out_shape=[shape((la...  15.9 us

profile of v2, /device:TPU:1, one launch (start us, length us, event | category | flops | bytes accessed | tf_op | source)
XLA Modules:
  0.0 174.0 jit_solution(7464970324300623561)
XLA Ops:
  0.6 157.3 %blocks.1 = (f32[128,256]{1,0:T(8,128)}, bf16[2,512,1024]{2,1,0:T(8,128)(2,1)}, bf16[2,1024,512]{2,1,0:T(8,128)(2,1)}, f32[2,256]{1,0:T(2,128)}, bf16[2,512,1024...) custom-call(f32[2,16,512]{2,1,0:T(8,128)} %refs_0_.1, ...), custom_call_target="tpu_custom_call" | custom-call | tf_op jit(solution)/shard_map/blocks/pallas_call | solution.py:1182
  157.9 15.9 %weight_grads.1 = (f32[16384,128]{1,0:T(8,128)}, f32[2,512,1024]{2,1,0:T(8,128)}, f32[128,256]{1,0:T(8,128)}, f32[128,256]{1,0:T(8,128)}, f32[2,256]{1,0:T(2,128...) custom-call(bf16[2,1024,1024]{2,1,0:T(8,128)(2,1)} %get-tuple-elemen, ...), custom_call_target="tpu_custom_call" | custom-call | tf_op jit(solution)/shard_map/weight_grads/pallas_call | solution.py:1264

commit v3 on v2

--- a/solution.py
+++ b/solution.py
@@ -52,7 +52,7 @@
     z.pack = 128
     assert max(z.xdim + z.taps + 1, z.rank + z.states + 2) <= z.pack
     z.shared = z.pack % (16 * z.ndp) == 0
-    z.piece = z.pack // z.ndp if z.shared else z.pack
+    z.piece = z.pack // z.ndp if z.shared else 16
     return z
 
 
@@ -83,8 +83,8 @@
         bce=vm((t, 2 * z.states, LANES), F32),
         dec=vm((t, z.states, c), F32),
         st=vm((t + 1, z.states, c), F32),
-        ssend=vm((8, c), F32),
-        ssum=vm((n, 8, c), F32),
+        ssend=vm((8, LANES), F32),
+        ssum=vm((n, 8, LANES), F32),
         carry=vm((2, z.states, c), BF16),
         sland=vm((n, z.states, c), BF16),
         rland=vm((n, z.states, c), BF16),
@@ -100,7 +100,8 @@
         g=vm((t, d), F32),
         packs=[vm((z.pack, c), F32) for _ in range(2)],
         packed=[vm((z.pack if z.shared else 16, c), BF16) for _ in range(2)],
-        rsland=[vm((n if z.shared else 1, z.piece, c), BF16) for _ in range(2)],
+        tland=[vm((z.pack // 2 if z.shared else 16, c), BF16) for _ in range(2)],
+        rsland=[vm((n // 2 if z.shared else 1, z.piece, c), BF16) for _ in range(2)],
         small=[vm((z.pack if z.shared else 16, c), BF16) for _ in range(2)],
         gnsend=vm((8, z.quarter), F32),
         gnland=vm((n, 8, z.quarter), F32),
@@ -269,35 +270,72 @@
 
         return arrive
 
+    ring = nq == 4
+    inner = (rank_q == 1) | (rank_q == 2)
+
     def gather(src, place, total):
-        first, second = alloc(1), alloc(1)
+        first, middle, second = alloc(1), alloc(1), alloc(1)
         local = pltpu.make_async_copy(src, place(dp), v.ls.at[alloc_local()])
         local.start()
-
-        def start(o, carry):
-            to = lax.rem(rank_q + o, nq) * 2 + pair
-            remote(src, place(dp), first, (to, ch)).start()
-            return carry
-
-        lax.fori_loop(1, nq, start, 0)
+        steps = (1, nq - 1) if ring else tuple(range(1, nq))
+        heard = len(steps)
+
+        def even(q):
+            return q * 2 + pair
+
+        def pass_on(q, to, index):
+            remote(place(even(q)), place(even(q)), index, to).start()
+
+        if ring:
+            for o in steps:
+                to = even(lax.rem(rank_q + o, nq))
+                remote(src, place(dp), first, (to, ch)).start()
+        else:
+
+            def start(o, carry):
+                to = even(lax.rem(rank_q + o, nq))
+                remote(src, place(dp), first, (to, ch)).start()
+                return carry
+
+            lax.fori_loop(1, nq, start, 0)
         remote(src, place(dp), second, (twin, ch)).start()
 
-        def forward():
-            bundle(total(nq - 1), first).wait_recv()
-
-            def body(o, carry):
-                origin = lax.rem(rank_q - o + nq, nq) * 2 + pair
-                remote(place(origin), place(origin), second, (twin, ch)).start()
-                return carry
-
-            lax.fori_loop(1, nq, body, 0)
+        def relay1():
+            bundle(total(heard), first).wait_recv()
+            if ring:
+
+                @pl.when(inner)
+                def _():
+                    pass_on(rank_q - 1, (even(rank_q + 1), ch), middle)
+                    pass_on(rank_q + 1, (even(rank_q - 1), ch), middle)
+
+                for o in steps:
+                    pass_on(lax.rem(rank_q + o, nq), (twin, ch), second)
+            else:
+
+                def body(o, carry):
+                    pass_on(lax.rem(rank_q + o, nq), (twin, ch), second)
+                    return carry
+
+                lax.fori_loop(1, nq, body, 0)
+
+        def relay2():
+            if ring:
+                bundle(total(1), middle).wait_recv()
+                pass_on(lax.rem(rank_q + 2, nq), (twin, ch), second)
 
         def finish():
-            bundle(total(nq - 1), first).wait_send()
+            bundle(total(heard), first).wait_send()
+            if ring:
+
+                @pl.when(inner)
+                def _():
+                    bundle(total(2), middle).wait_send()
+
             bundle(total(nq), second).wait()
             local.wait()
 
-        return SimpleNamespace(forward=forward, finish=finish)
+        return SimpleNamespace(relay1=relay1, relay2=relay2, finish=finish)
 
     locals_used = [2 * z.layers + 10]
 
@@ -476,9 +514,10 @@
         L[l].step[...] = step
         L[l].stepk[...] = stepk
         L[l].u[...] = step * L[l].actf[...]
-        L[l].ssend[...] = jnp.broadcast_to(
-            jnp.sum(stepk, axis=0, keepdims=True), (8, c)
-        )
+        summed = jnp.sum(stepk, axis=0, keepdims=True)
+        L[l].ssend[...] = jnp.zeros((8, LANES), F32)
+        for g in range(groups):
+            L[l].ssend[g : g + 1, :] = summed[:, lane(g)]
         land = L[l].ssum
         got_s = dp_send_all(lambda to: L[l].ssend, land.at[dp], land.at[0 : n - 1])
         bc = proj[rank : rank + 2 * ns, :]
@@ -545,9 +584,10 @@
 
         def body(k, carry):
             j = order(k)
-            return (
-                jnp.exp(a * L[l].ssum[j, 0:1, :]) * carry + land[j].astype(F32)
+            row = jnp.concatenate(
+                [L[l].ssum[j, g : g + 1, :] for g in range(groups)], axis=1
             )
+            return jnp.exp(a * row) * carry + land[j].astype(F32)
 
         return lax.fori_loop(0, count, body, jnp.zeros((ns, c), F32))
 
@@ -807,41 +847,68 @@
         )
         v.gains[l : l + 1, :] = total[0:1, :]
 
-    def small_scatter(l, p):
+    def rows_of(first, count):
+        return pl.ds(pl.multiple_of(first, count), count)
+
+    def small_sum(l, p):
         if not z.shared:
             v.smalls[l, p] = L[l].packs[p][...]
-            return None
-        rows = z.piece
-        packed, land = L[l].packed[p], L[l].rsland[p]
-        packed[...] = L[l].packs[p][...].astype(BF16)
-        piece = lambda j: pl.ds(pl.multiple_of(j * rows, rows), rows)
-        arrive = dp_send_all(
-            lambda to: packed.at[piece(to), :], land.at[dp], land.at[0 : n - 1]
-        )
-        land[dp] = packed[piece(dp), :]
-        return arrive
-
-    def small_gather(l, p, arrive):
-        if not z.shared:
-            return None
-        rows = z.piece
-        small, land = L[l].small[p], L[l].rsland[p]
-        arrive()
-        total = lax.fori_loop(
-            0, n, lambda j, s: s + land[j].astype(F32), jnp.zeros((rows, c), F32)
-        )
-        mine = pl.ds(pl.multiple_of(dp * rows, rows), rows)
-        small[mine, :] = total.astype(BF16)
-        return dp_send_all(
-            lambda to: small.at[mine, :],
-            small.at[mine, :],
-            small.at[0 : (n - 1) * rows, :],
-        )
-
-    def small_out(l, p, arrive):
-        if z.shared:
-            arrive()
-            v.smalls[l, p] = L[l].small[p][...]
+            nothing = lambda: None
+            return SimpleNamespace(b=nothing, c=nothing, d=nothing, out=nothing)
+        rows, part = z.piece, z.pack // 2
+        pack, packed, tland = L[l].packs[p], L[l].packed[p], L[l].tland[p]
+        land, small = L[l].rsland[p], L[l].small[p]
+        mine, other = rows_of(pair * part, part), rows_of((1 - pair) * part, part)
+        place = rows_of(pair * part + rank_q * rows, rows)
+        packed[other, :] = pack[other, :].astype(BF16)
+        got_a = send(packed.at[other, :], tland, (twin, ch))
+        state = {}
+
+        def even_send(src_of, dst, total):
+            index = alloc(1)
+
+            def body(o, carry):
+                q = lax.rem(rank_q + o, nq)
+                remote(src_of(q), dst, index, (q * 2 + pair, ch)).start()
+                return carry
+
+            lax.fori_loop(1, nq, body, 0)
+            whole = bundle(total, index)
+            drains.append(whole.wait_send)
+            return whole
+
+        def b():
+            got_a.wait_recv()
+            packed[mine, :] = (pack[mine, :] + tland[...].astype(F32)).astype(BF16)
+            piece = lambda q: rows_of(pair * part + q * rows, rows)
+            state[0] = even_send(
+                lambda q: packed.at[piece(q), :],
+                land.at[rank_q],
+                land.at[0 : nq - 1],
+            )
+            land[rank_q] = packed[place, :]
+
+        def c_():
+            state[0].wait_recv()
+            total = land[0].astype(F32)
+            for k in range(1, nq):
+                total = total + land[k].astype(F32)
+            small[place, :] = total.astype(BF16)
+            state[1] = even_send(
+                lambda q: small.at[place, :],
+                small.at[place, :],
+                small.at[0 : (nq - 1) * rows, :],
+            )
+
+        def d_():
+            state[1].wait_recv()
+            state[2] = send(small.at[mine, :], small.at[mine, :], (twin, ch))
+
+        def out():
+            state[2].wait_recv()
+            v.smalls[l, p] = small[...]
+
+        return SimpleNamespace(b=b, c=c_, d=d_, out=out)
 
     def inverse(total):
         return lax.rsqrt(total * (1.0 / d) + EPSILON)
@@ -1021,14 +1088,16 @@
     loads[0][1].wait()
     got_s0()
     got_carry(1, dp + 1)
-    hid0.forward()
-    gq1.forward()
+    hid0.relay1()
+    gq1.relay1()
     scan_out(0, carry_in(0, L[0].sland, lambda k: k, dp))
     scan0 = gather_scan(0)
     red0 = reduce_a(0, out_part(0))
     red0, arrive = reduce_b(0, red0, True)
     share_g = share_g()
     got_c = reduce_c(0, red0, arrive)
+    hid0.relay2()
+    gq1.relay2()
     share_x()
     got_xedge()
     got_c.wait_recv()
@@ -1040,13 +1109,16 @@
 
     got_p = fwd_head(1)
     hid1 = gather_hid(1)
-    scan0.forward()
+    scan0.relay1()
     loads[1][1].wait()
     share_c()
     back_gate(1)
     got_s1 = fwd_mid(1, got_p)
+    scan0.relay2()
     hid0.finish()
     share0 = share_hid(0)
+    gq1.finish()
+    share1 = share_gq(1)
     put(L[1].carry, 0, scan_sum(1))
     put(L[1].carry, 1, back_sum(1))
     base = alloc(n - 1)
@@ -1055,84 +1127,100 @@
     got_s1()
     got_f(1, dp + 1)
     got_r(dp + 1, n)
-    hid1.forward()
-    gq1.finish()
-    share1 = share_gq(1)
+    hid1.relay1()
     scan_out(1, carry_in(1, L[1].sland, lambda k: k, dp))
     scan1 = gather_scan(1)
     back_dgate(1)
     red1 = reduce_a(1, out_part(1))
+    hid1.relay2()
 
     acc_b, acc_c = back_scan(1, carry_in(1, L[1].rland, lambda k: n - 1 - k, n - 1 - dp))
     got_b, edge = back_mid(1, acc_b, acc_c)
     share0 = share0()
-    red1, _ = reduce_b(1, red1, False)
+    share1 = share1()
+    scan1.relay1()
     dproj = back_conv(1, got_b, edge)
     red2 = reduce_a(2, in_part(1))
     dmi1 = gather_dmi(1)
     back_rest(1, dproj)
     red2, _ = reduce_b(2, red2, False)
-    share1 = share1()
-    reduce_c(1, red1, None).wait_recv()
-    share1()
-    v.block_out[...] = L[1].xs[own, q_cols] + R[1].full[own, q_cols]
-    scan1.forward()
-    reduce_c(2, red2, None).wait_recv()
+    red1, _ = reduce_b(1, red1, False)
+    scan1.relay2()
+    red2 = reduce_c(2, red2, None)
+    hid1.finish()
     share_g()
+    red2.wait_recv()
+    share2 = share_hid(1)
     grad, gain1 = back_norm(1, 2)
     L[0].g[...] = grad
     L[0].gq[...] = grad.astype(BF16)
 
+    gq0 = gather_gq(0)
     back_gate(0)
     put(L[0].carry, 1, back_sum(0))
     got_r = dp_send(L[0].carry.at[1], L[0].rland.at[dp], alloc(n - 1), n - dp, n)
+    gq0.relay1()
     back_dgate(0)
-    hid1.finish()
-    share2 = share_hid(1)
+    reduce_c(1, red1, None).wait_recv()
+    v.block_out[...] = L[1].xs[own, q_cols] + R[1].full[own, q_cols]
+    share0()
+    share1()
     got_r(dp + 1, n)
-    gq0 = gather_gq(0)
-    dmi1.forward()
-    small1 = [small_scatter(1, 0), small_scatter(1, 1)]
+    gq0.relay2()
+    dmi1.relay1()
+    small1 = [small_sum(1, 0), small_sum(1, 1)]
     acc_b, acc_c = back_scan(0, carry_in(0, L[0].rland, lambda k: n - 1 - k, n - 1 - dp))
     got_b, edge = back_mid(0, acc_b, acc_c)
     share2 = share2()
-    small0 = [small_scatter(0, 0)]
-    gq0.forward()
-    dproj = back_conv(0, got_b, edge)
-    dmi0 = [gather_dmi(0, 0, t // 2), gather_dmi(0, t // 2, t)]
-    red3 = reduce_a(3, in_part(0))
-    back_rest(0, dproj)
-    small0.append(small_scatter(0, 1))
-    red3, _ = reduce_b(3, red3, False)
-    small1 = [small_gather(1, p, small1[p]) for p in range(2)]
+    small0 = [small_sum(0, 0)]
+    dmi1.relay2()
     share2()
     scan1.finish()
     finish_begin(1)
     gq0.finish()
+    finish_some(1, 0, chunks // 2)
+    dproj = back_conv(0, got_b, edge)
+    dmi0 = [gather_dmi(0, 0, t // 2), gather_dmi(0, t // 2, t)]
     share3 = share_gq(0)
-    finish_some(1, 0, chunks // 2)
+    red3 = reduce_a(3, in_part(0))
+    back_rest(0, dproj)
+    small0.append(small_sum(0, 1))
+    for one in small1:
+        one.b()
+    small0[0].b()
+    red3, _ = reduce_b(3, red3, False)
+    finish_some(1, chunks // 2, 3 * chunks // 4)
+    small0[1].b()
+    dmi0[0].relay1()
+    for one in small1:
+        one.c()
+    small0[0].c()
+    finish_some(1, 3 * chunks // 4, chunks)
+    dmi0[1].relay1()
     got_c = reduce_c(3, red3, None)
-    finish_some(1, chunks // 2, chunks)
+    small0[1].c()
+    share3 = share3()
     got_c.wait_recv()
     grad, gain0 = back_norm(0, 3)
     L[0].g[...] = grad
     v.input_grad[...] = L[0].g[:, q_cols]
-    dmi0[0].forward()
-    share3 = share3()
-    share0()
+    dmi0[0].relay2()
     scan0.finish()
+    finish_end(1)
     share3()
-    finish_end(1)
     finish_begin(0)
-    small0 = [small_gather(0, p, small0[p]) for p in range(2)]
-    dmi0[1].forward()
-    finish_some(0, 0, chunks)
-    finish_end(0)
+    for one in small1:
+        one.d()
+    small0[0].d()
+    finish_some(0, 0, chunks // 2)
+    dmi0[1].relay2()
+    small0[1].d()
+    finish_some(0, chunks // 2, chunks)
     gain_out(0, gain0)
     gain_out(1, gain1)
-    for p in range(2):
-        small_out(1, p, small1[p])
-        small_out(0, p, small0[p])
+    for one in small0 + small1:
+        one.out()
+    finish_end(0)
     for one in (dmi1, *dmi0):
         one.finish()
     for drain in drains:
@@ -1141,7 +1229,7 @@
 
 
 def run_blocks(z, args):
-    sems = (62 + 3 * (z.ndp - 1) + (8 if z.shared else 0), 23)
+    sems = (71 + 3 * (z.ndp - 1) + (16 if z.shared else 0), 23)
     vmem = pl.BlockSpec(memory_space=pltpu.VMEM)
     smem = pl.BlockSpec(memory_space=pltpu.SMEM)
     anywhere = pl.BlockSpec(memory_space=pl.ANY)
@@ -1214,23 +1302,69 @@
         wout[0] = jnp.where(first, 0.0, wout[0]) + part
 
     begin = first & (pl.program_id(0) == 0) & (pl.program_id(1) == 0)
-
-    @pl.when(begin)
-    def _():
-        for src, to in zip(small_ins, outs[:3], strict=True):
-            to[...] = src[...]
-        at, pack = 0, 0
-        for i, to in enumerate(outs[3:]):
-            if i == 4:
-                at, pack = 0, 1
-            for l in range(z.layers):
-                if len(to.shape) == 3:
-                    count = to.shape[1]
-                    to[l] = smalls[l, pack, at : at + count, :].astype(F32)
+    pl.when(begin)(lambda: small_outputs(z, smalls, small_ins, outs))
+
+
+def small_outputs(z, smalls, small_ins, outs):
+    for src, to in zip(small_ins, outs[:3], strict=True):
+        to[...] = src[...]
+    at, pack = 0, 0
+    for i, to in enumerate(outs[3:]):
+        if i == 4:
+            at, pack = 0, 1
+        for l in range(z.layers):
+            if len(to.shape) == 3:
+                count = to.shape[1]
+                to[l] = smalls[l, pack, at : at + count, :].astype(F32)
+            else:
+                count = 1
+                to[l : l + 1, :] = smalls[l, pack, at : at + 1, :].astype(F32)
+        at += count
+
+
+def grads_at_once(z, ins, small_ins, win, wout, outs, *scratch):
+    smalls = ins[5]
+    held, (winv, woutv, lsem, ssem) = scratch[:5], scratch[5:]
+    layers, d, c = z.layers, z.width, z.chans
+    hid, gat, dmg, gq, dmi = held
+    loads = {}
+    for l in range(layers):
+        for i in (1, 3, 0, 4, 2):
+            copy = pltpu.make_async_copy(ins[i].at[l], held[i].at[l], lsem.at[5 * l + i])
+            copy.start()
+            loads[l, i] = copy
+    small_outputs(z, smalls, small_ins, outs)
+    stores = []
+
+    def leave(src, to):
+        copy = pltpu.make_async_copy(src, to, ssem.at[len(stores)])
+        copy.start()
+        stores.append(copy)
+
+    rows = d // 2
+    for l in range(layers):
+        loads[l, 1].wait()
+        loads[l, 3].wait()
+        woutv[l] = dot(gat[l], gq[l])
+        leave(woutv.at[l], wout.at[l])
+        loads[l, 0].wait()
+        loads[l, 4].wait()
+        loads[l, 2].wait()
+        for half in range(2):
+            lhs = hid[l, half * rows : (half + 1) * rows, :]
+            base = (l * d + half * rows) * z.span
+            for k in range(2):
+                if k == 0:
+                    part = dot(lhs, dmi[l])
                 else:
-                    count = 1
-                    to[l : l + 1, :] = smalls[l, pack, at : at + 1, :].astype(F32)
-            at += count
+                    part = dot(lhs, dmg[l], ((1,), (1,)))
+                for j in range(z.groups):
+                    at = pl.ds(base + j * 2 + k, rows, stride=z.span)
+                    winv[at, :] = part[:, j * LANES : (j + 1) * LANES]
+            span = pl.ds(base, rows * z.span)
+            leave(winv.at[span, :], win.at[span, :])
+    for copy in stores:
+        copy.wait()
 
 
 def weight_grads(z, r):
@@ -1258,18 +1392,38 @@
         return pl.BlockSpec(one.shape, lambda l, i, k: (0,) * dims)
 
     def kernel(*refs):
-        ins, small_ins, (win, wout), outs = refs[:6], refs[6:9], refs[9:11], refs[11:]
-        grad_kernel(z, steps, ins, small_ins, win, wout, outs)
-
-    win, wout, *rest = pl.pallas_call(
-        kernel,
-        grid=(layers, blocks, steps),
-        out_shape=[
-            shape((layers * d * z.span, LANES), F32),
-            shape((layers, c, d), F32),
-            *[shape(one.shape, F32) for one in small_shapes],
-        ],
-        in_specs=[
+        ins, small_ins, (win, wout), rest = refs[:6], refs[6:9], refs[9:11], refs[11:]
+        outs = rest[: len(small_shapes)]
+        if steps == 1:
+            scratch = rest[len(small_shapes) :]
+            grads_at_once(z, ins, small_ins, win, wout, outs, *scratch)
+        else:
+            grad_kernel(z, steps, ins, small_ins, win, wout, outs)
+
+    out_shape = [
+        shape((layers * d * z.span, LANES), F32),
+        shape((layers, c, d), F32),
+        *[shape(one.shape, F32) for one in small_shapes],
+    ]
+    in_specs, out_specs, scratch, grid = None, None, (), (layers, blocks, steps)
+    if steps == 1:
+        grid = ()
+        anywhere = [pl.BlockSpec(memory_space=pl.ANY)]
+        vmem = [pl.BlockSpec(memory_space=pltpu.VMEM)]
+        in_specs = anywhere * 5 + vmem * 4
+        out_specs = anywhere * 2 + vmem * len(small_shapes)
+        scratch = (
+            *[
+                pltpu.VMEM(one.shape, BF16)
+                for one in (r.hid_all, r.gat_all, r.dmg_all, r.gq_all, r.dmi_all)
+            ],
+            pltpu.VMEM(out_shape[0].shape, F32),
+            pltpu.VMEM(out_shape[1].shape, F32),
+            pltpu.SemaphoreType.DMA((5 * layers,)),
+            pltpu.SemaphoreType.DMA((3 * layers,)),
+        )
+    else:
+        in_specs = [
             pl.BlockSpec((1, rows, deep), lambda l, i, k: (l, i, k)),
             pl.BlockSpec((1, orow, deep), lambda l, i, k: (l, i, k)),
             pl.BlockSpec((1, c, deep), lambda l, i, k: (l, 0, k)),
@@ -1279,12 +1433,19 @@
             fixed(r.block_out),
             fixed(r.input_grad),
             fixed(r.gains),
-        ],
-        out_specs=[
+        ]
+        out_specs = [
             pl.BlockSpec((rows * z.span, LANES), lambda l, i, k: (l * blocks + i, 0)),
             pl.BlockSpec((1, orow, d), lambda l, i, k: (l, i, 0)),
             *[fixed(one) for one in small_shapes],
-        ],
+        ]
+    win, wout, *rest = pl.pallas_call(
+        kernel,
+        grid=grid,
+        out_shape=out_shape,
+        in_specs=in_specs,
+        out_specs=out_specs,
+        scratch_shapes=scratch,
         compiler_params=pltpu.CompilerParams(vmem_limit_bytes=60 * 2**20),
         name="weight_grads",
     )(

time: 174 us -> 155 us (0.89)
  Pallas kernels: 173 us -> 154 us
    pallas_call x1, Pallas kernels: 157 us -> 140 us  [run_blocks(): pl.pallas_call(kernel, out_shape=[one[0] for one in trees[1][0]], in_spec...]
    pallas_call x1, Pallas kernels: 15.9 us -> 13.1 us  [weight_grads(): pl.pallas_call(kernel, grid=grid, out_shape=out_shape, in_specs=in_specs,...]
where the time goes in v3:
time: 155 us; the launch traced here: 154 us
  Pallas kernels  154 us (99%)
    pallas_call x1, Pallas kernels, run_blocks(): pl.pallas_call(kernel, out_shape=[one[0] for one in trees[1][0]], in_spec...  140 us
    pallas_call x1, Pallas kernels, weight_grads(): pl.pallas_call(kernel, grid=grid, out_shape=out_shape, in_specs=in_specs,...  13.1 us

profile of v3, /device:TPU:1, one launch (start us, length us, event | category | flops | bytes accessed | tf_op | source)
XLA Modules:
  0.0 154.4 jit_solution(3529346452188389383)
XLA Ops:
  0.6 140.4 %blocks.1 = (f32[128,256]{1,0:T(8,128)}, bf16[2,512,1024]{2,1,0:T(8,128)(2,1)}, bf16[2,1024,512]{2,1,0:T(8,128)(2,1)}, f32[2,256]{1,0:T(2,128)}, bf16[2,512,1024...) custom-call(f32[2,16,512]{2,1,0:T(8,128)} %refs_0_.1, ...), custom_call_target="tpu_custom_call" | custom-call | tf_op jit(solution)/shard_map/blocks/pallas_call | solution.py:1270
  141.1 13.1 %weight_grads.1 = (f32[16384,128]{1,0:T(8,128)}, f32[2,512,1024]{2,1,0:T(8,128)}, f32[128,256]{1,0:T(8,128)}, f32[128,256]{1,0:T(8,128)}, f32[2,256]{1,0:T(2,128...) custom-call(bf16[2,1024,1024]{2,1,0:T(8,128)(2,1)} %get-tuple-elemen, ...), custom_call_target="tpu_custom_call" | custom-call | tf_op jit(solution)/shard_map/weight_grads/pallas_call | solution.py:1442

commit v4 on v3

--- a/solution.py
+++ b/solution.py
@@ -26,6 +26,10 @@
 
 def silu_slope(value, sig):
     return sig * (1.0 + value * (1.0 - sig))
+
+
+def side_by_side(parts):
+    return jnp.concatenate([parts[k] for k in range(parts.shape[0])], axis=1)
 
 
 def wide(column, width):
@@ -91,8 +95,8 @@
         bsend=vm((z.xdim, t), BF16),
         bland=vm((z.nch, z.xdim, t), BF16),
         bhalo=vm((z.nch, z.xdim, t), BF16),
-        esend=vm((2 * HALO, c), F32),
-        eland=vm((2 * HALO, c), F32),
+        esend=vm((2 * ROWS, c), F32),
+        eland=vm((2 * ROWS, c), F32),
         dm=vm((t, 2 * c), BF16),
         ht=vm((z.quarter, t), BF16),
         sct=vm((c, t), BF16),
@@ -135,7 +139,7 @@
         raw=vm((d * z.span, LANES), BF16),
         stage=vm((LANES * z.span, LANES), F32),
         hidc=vm((2, d, z.chunk), BF16),
-        gqc=vm((2, z.chunk, d), BF16),
+        gqc=vm((2, z.nch, z.chunk, z.quarter), BF16),
         scanc=vm((2, c, z.chunk), BF16),
         gatc=vm((2, c, z.chunk), BF16),
         dmgc=vm((2, c, z.chunk), BF16),
@@ -766,8 +770,8 @@
         land[ch] = bsend[...]
         dact = ds * v.skip[l : l + 1, :] + L[l].step[...] * v.adj[...]
         v.dact[...] = dact
-        L[l].esend[0:HALO, :] = dact[0:HALO, :]
-        L[l].esend[HALO : 2 * HALO, :] = L[l].slope[0:HALO, :]
+        L[l].esend[0:ROWS, :] = dact[0:ROWS, :]
+        L[l].esend[ROWS : 2 * ROWS, :] = L[l].slope[0:ROWS, :]
         edge = edge_send(
             [
                 ([(L[l].esend, L[l].eland, ch)], L[l].eland),
@@ -798,8 +802,8 @@
         dconv = dact * L[l].slope[...]
         v.dc[0:t, :] = dconv
         eland = L[l].eland
-        after = dot(dproj_h, wx, ((0,), (0,)))[0:HALO, :]
-        v.dc[t:ext, :] = (eland[0:HALO, :] + after) * eland[HALO : 2 * HALO, :]
+        after = dot(dproj_h, wx, ((0,), (0,)))[0:ROWS, :]
+        v.dc[t : t + ROWS, :] = (eland[0:ROWS, :] + after) * eland[ROWS : 2 * ROWS, :]
         dinner = jnp.zeros((t, c), F32)
         for k in range(z.taps):
             at = z.taps - 1 - k
@@ -934,12 +938,12 @@
             lambda count: ref.at[l, rows, 0 : count * t],
         )
 
-    def in_rows(src, ref, l, cols, low=0, high=t):
+    def in_rows(src, ref, low=0, high=t):
         m = high - low
         return gather(
             src,
-            lambda j: ref.at[l, pl.ds(pl.multiple_of(j * t + low, m), m), cols],
-            lambda count: ref.at[l, 0 : count * m, cols],
+            lambda j: ref.at[pl.ds(pl.multiple_of(j * t + low, m), m), :],
+            lambda count: ref.at[0 : count * m, :],
         )
 
     def gather_hid(l):
@@ -954,11 +958,11 @@
         return in_lanes(L[l].sct, v.scan_all, l, slice(None))
 
     def gather_gq(l):
-        return in_rows(L[l].gq.at[:, q_cols], v.gq_all, l, q_cols)
+        return in_rows(L[l].gq.at[:, q_cols], v.gq_all.at[l, ch])
 
     def gather_dmi(l, low=0, high=t):
         src = L[l].dm.at[low:high, 0:c]
-        return in_rows(src, v.dmi_all, l, slice(None), low, high)
+        return in_rows(src, v.dmi_all.at[l], low, high)
 
     def quarter_at(k):
         return pl.ds(pl.multiple_of(k * quarter, quarter), quarter)
@@ -983,8 +987,8 @@
 
     def share_gq(l):
         return share(
-            lambda k: v.gq_all.at[l, :, quarter_at(k)],
-            v.gq_all.at[l, :, 0 : 2 * quarter],
+            lambda k: v.gq_all.at[l, k],
+            v.gq_all.at[l, 0:2],
         )
 
     def share_rows(ref, rows):
@@ -998,7 +1002,7 @@
         at = pl.ds(pl.multiple_of(k * z.chunk, z.chunk), z.chunk)
         pairs = (
             (v.hid_all.at[l, :, at], v.hidc.at[slot]),
-            (v.gq_all.at[l, at, :], v.gqc.at[slot]),
+            (v.gq_all.at[l, :, at, :], v.gqc.at[slot]),
             (v.scan_all.at[l, :, at], v.scanc.at[slot]),
         )
         return [
@@ -1042,7 +1046,7 @@
             w_gate = v.wi[l, :, c : 2 * c]
             gate = dot(w_gate, v.hidc[slot], ((0,), (0,))).astype(BF16).astype(F32)
             loads_in[1].wait()
-            dgated = dot(v.wo[l], v.gqc[slot], ((1,), (1,)))
+            dgated = dot(v.wo[l], side_by_side(v.gqc[slot]), ((1,), (1,)))
             loads_in[2].wait()
             scanned = v.scanc[slot].astype(F32)
             sig = jax.nn.sigmoid(gate)
@@ -1059,12 +1063,16 @@
             for copy in chunk_stores(l, jnp.int32(k)):
                 copy.wait()
 
+    gq1 = gather_gq(1)
     load_in(0)
     got_h.wait_recv()
     got_m.wait_recv()
     got_edge()
     norms()
+    gq1.relay1()
+    hid0 = gather_hid(0)
     got_p = fwd_head(0)
+    gq1.relay2()
     share_x = share_rows(L[0].xs, own)
     share_c = share_rows(L[1].gq, slice(None))
     got_xedge = edge_send(
@@ -1076,28 +1084,24 @@
         ],
         1,
     )
-    hid0 = gather_hid(0)
-    gq1 = gather_gq(1)
     load_in(1)
     got_s0 = fwd_mid(0, got_p)
     put(L[0].carry, 0, scan_sum(0))
     got_carry = dp_send(L[0].carry.at[0], L[0].sland.at[dp], alloc(n - 1), 1, n - dp)
+    gq1.finish()
+    share1 = share_gq(1)
     share_x = share_x()
     share_c = share_c()
-    share_g = share_rows(L[1].g, slice(None))
     loads[0][1].wait()
     got_s0()
     got_carry(1, dp + 1)
     hid0.relay1()
-    gq1.relay1()
     scan_out(0, carry_in(0, L[0].sland, lambda k: k, dp))
     scan0 = gather_scan(0)
     red0 = reduce_a(0, out_part(0))
     red0, arrive = reduce_b(0, red0, True)
-    share_g = share_g()
     got_c = reduce_c(0, red0, arrive)
     hid0.relay2()
-    gq1.relay2()
     share_x()
     got_xedge()
     got_c.wait_recv()
@@ -1109,16 +1113,15 @@
 
     got_p = fwd_head(1)
     hid1 = gather_hid(1)
-    scan0.relay1()
     loads[1][1].wait()
     share_c()
     back_gate(1)
+    scan0.relay1()
     got_s1 = fwd_mid(1, got_p)
     scan0.relay2()
     hid0.finish()
     share0 = share_hid(0)
-    gq1.finish()
-    share1 = share_gq(1)
+    share1 = share1()
     put(L[1].carry, 0, scan_sum(1))
     put(L[1].carry, 1, back_sum(1))
     base = alloc(n - 1)
@@ -1130,20 +1133,20 @@
     hid1.relay1()
     scan_out(1, carry_in(1, L[1].sland, lambda k: k, dp))
     scan1 = gather_scan(1)
+    share_g = share_rows(L[1].g, slice(None))
     back_dgate(1)
     red1 = reduce_a(1, out_part(1))
     hid1.relay2()
 
     acc_b, acc_c = back_scan(1, carry_in(1, L[1].rland, lambda k: n - 1 - k, n - 1 - dp))
     got_b, edge = back_mid(1, acc_b, acc_c)
-    share0 = share0()
-    share1 = share1()
     scan1.relay1()
     dproj = back_conv(1, got_b, edge)
     red2 = reduce_a(2, in_part(1))
     dmi1 = gather_dmi(1)
     back_rest(1, dproj)
     red2, _ = reduce_b(2, red2, False)
+    share_g = share_g()
     red1, _ = reduce_b(1, red1, False)
     scan1.relay2()
     red2 = reduce_c(2, red2, None)
@@ -1163,33 +1166,32 @@
     back_dgate(0)
     reduce_c(1, red1, None).wait_recv()
     v.block_out[...] = L[1].xs[own, q_cols] + R[1].full[own, q_cols]
-    share0()
-    share1()
+    share0 = share0()
     got_r(dp + 1, n)
     gq0.relay2()
     dmi1.relay1()
-    small1 = [small_sum(1, 0), small_sum(1, 1)]
     acc_b, acc_c = back_scan(0, carry_in(0, L[0].rland, lambda k: n - 1 - k, n - 1 - dp))
     got_b, edge = back_mid(0, acc_b, acc_c)
     share2 = share2()
+    small1 = [small_sum(1, 0), small_sum(1, 1)]
     small0 = [small_sum(0, 0)]
     dmi1.relay2()
+    share1()
     share2()
     scan1.finish()
     finish_begin(1)
     gq0.finish()
-    finish_some(1, 0, chunks // 2)
     dproj = back_conv(0, got_b, edge)
     dmi0 = [gather_dmi(0, 0, t // 2), gather_dmi(0, t // 2, t)]
     share3 = share_gq(0)
-    red3 = reduce_a(3, in_part(0))
     back_rest(0, dproj)
     small0.append(small_sum(0, 1))
+    red3 = reduce_a(3, in_part(0))
     for one in small1:
         one.b()
     small0[0].b()
     red3, _ = reduce_b(3, red3, False)
-    finish_some(1, chunks // 2, 3 * chunks // 4)
+    finish_some(1, 0, 3 * chunks // 4)
     small0[1].b()
     dmi0[0].relay1()
     for one in small1:
@@ -1207,6 +1209,7 @@
     dmi0[0].relay2()
     scan0.finish()
     finish_end(1)
+    share0()
     share3()
     finish_begin(0)
     for one in small1:
@@ -1247,7 +1250,7 @@
         gat_all=(shape((layers, c, n), BF16), anywhere),
         dmg_all=(shape((layers, c, n), BF16), anywhere),
         scan_all=(shape((layers, c, n), BF16), anywhere),
-        gq_all=(shape((layers, n, d), BF16), anywhere),
+        gq_all=(shape((layers, z.nch, n, z.quarter), BF16), anywhere),
         dmi_all=(shape((layers, n, c), BF16), anywhere),
     )
     scratch = scratch_of(z)
@@ -1295,7 +1298,7 @@
                 win[at, :] = piece
             else:
                 win[at, :] = jnp.where(first, 0.0, win[at, :]) + piece
-    part = dot(gat[0], gq[0])
+    part = dot(gat[0], side_by_side(gq[0]))
     if steps == 1:
         wout[0] = part
     else:
@@ -1345,7 +1348,7 @@
     for l in range(layers):
         loads[l, 1].wait()
         loads[l, 3].wait()
-        woutv[l] = dot(gat[l], gq[l])
+        woutv[l] = dot(gat[l], side_by_side(gq[l]))
         leave(woutv.at[l], wout.at[l])
         loads[l, 0].wait()
         loads[l, 4].wait()
@@ -1427,7 +1430,7 @@
             pl.BlockSpec((1, rows, deep), lambda l, i, k: (l, i, k)),
             pl.BlockSpec((1, orow, deep), lambda l, i, k: (l, i, k)),
             pl.BlockSpec((1, c, deep), lambda l, i, k: (l, 0, k)),
-            pl.BlockSpec((1, deep, d), lambda l, i, k: (l, k, 0)),
+            pl.BlockSpec((1, z.nch, deep, z.quarter), lambda l, i, k: (l, 0, k, 0)),
             pl.BlockSpec((1, deep, c), lambda l, i, k: (l, k, 0)),
             fixed(r.smalls),
             fixed(r.block_out),

time: 155 us -> 144 us (0.929)
  Pallas kernels: 154 us -> 143 us
    pallas_call x1, Pallas kernels: 140 us -> 130 us  [run_blocks(): pl.pallas_call(kernel, out_shape=[one[0] for one in trees[1][0]], in_spec...]
where the time goes in v4:
time: 144 us
  Pallas kernels  143 us (99%)
    pallas_call x1, Pallas kernels, run_blocks(): pl.pallas_call(kernel, out_shape=[one[0] for one in trees[1][0]], in_spec...  130 us
    pallas_call x1, Pallas kernels, weight_grads(): pl.pallas_call(kernel, grid=grid, out_shape=out_shape, in_specs=in_specs,...  13.1 us

profile of v4, /device:TPU:1, one launch (start us, length us, event | category | flops | bytes accessed | tf_op | source)
XLA Modules:
  0.0 143.8 jit_solution(13571324412145739149)
XLA Ops:
  0.6 129.9 %blocks.1 = (f32[128,256]{1,0:T(8,128)}, bf16[2,512,1024]{2,1,0:T(8,128)(2,1)}, bf16[2,1024,512]{2,1,0:T(8,128)(2,1)}, f32[2,256]{1,0:T(2,128)}, bf16[2,512,1024...) custom-call(f32[2,16,512]{2,1,0:T(8,128)} %refs_0_.1, ...), custom_call_target="tpu_custom_call" | custom-call | tf_op jit(solution)/shard_map/blocks/pallas_call | solution.py:1273
  130.5 13.1 %weight_grads.1 = (f32[16384,128]{1,0:T(8,128)}, f32[2,512,1024]{2,1,0:T(8,128)}, f32[128,256]{1,0:T(8,128)}, f32[128,256]{1,0:T(8,128)}, f32[2,256]{1,0:T(2,128...) custom-call(bf16[2,1024,1024]{2,1,0:T(8,128)(2,1)} %get-tuple-elemen, ...), custom_call_target="tpu_custom_call" | custom-call | tf_op jit(solution)/shard_map/weight_grads/pallas_call | solution.py:1445
